TPU v7x, 512 devices: a whole 4x8x8 slice. The times are simulated.
512 devices in a mesh: section: 8 (over z), node: 8 (over x, core), local: 8 (over y).
Axes of the slice: x: 4, y: 8, z: 8, core: 2. Of those that a mesh axis runs over, the one named last changes fastest.
Arguments:
- section_inputs: bfloat16 [8, 64, 4, 196, 512], P('section', ('node', 'local')), may hold values from -6 to 6
- grad_in: bfloat16 [8, 64, 196, 512], P('section', ('node', 'local')), may hold values from -6 to 6
- loss_grad: bfloat16 [64, 3, 196, 512], P(('node', 'local')), may hold values from -6 to 6
- w_reduce: bfloat16 [8, 512, 256], P('section'), may hold values from -0.25 to 0.25
- w_spatial: bfloat16 [8, 2304, 256], P('section'), may hold values from -0.125 to 0.125
- w_expand: bfloat16 [8, 256, 512], P('section'), may hold values from -0.375 to 0.375
- err_reduce: bfloat16 [8, 64, 512, 256], P('section', ('node', 'local')), may hold values from -360 to 360
- err_spatial: bfloat16 [8, 64, 2304, 256], P('section', ('node', 'local')), may hold values from -360 to 360
- err_expand: bfloat16 [8, 64, 256, 512], P('section', ('node', 'local')), may hold values from -360 to 360
- prior_reduce: float32 [8, 32, 256], P('section'), may hold values from -6 to 6
- prior_spatial: float32 [8, 32, 256], P('section'), may hold values from -6 to 6
- prior_expand: float32 [8, 32, 512], P('section'), may hold values from -6 to 6
Outputs:
- leaving: bfloat16 [8, 64, 196, 512], P('section', ('node', 'local'))
- basis_reduce: float32 [8, 32, 512], P('section', None, ('node', 'local'))
- basis_spatial: float32 [8, 32, 2304], P('section', None, ('node', 'local'))
- basis_expand: float32 [8, 32, 256], P('section', None, ('node', 'local'))
- right_reduce: float32 [8, 32, 256], P('section', None, ('node', 'local'))
- right_spatial: float32 [8, 32, 256], P('section', None, ('node', 'local'))
- right_expand: float32 [8, 32, 512], P('section', None, ('node', 'local'))
All inputs are finite; a program needn't handle non-finite values.
Results may differ from a plain program's by a relative error of at most 0.0095.
Values may be sent and summed in bfloat16 or wider, within the bound.
A program may use at most 128 MiB of HBM per device.

v0:
```python
import math

import jax
import jax.numpy as jnp
from jax import lax
from jax.sharding import PartitionSpec as P

SIDE = 14


precise = lax.Precision.HIGHEST


def shifted_2(block, axis, distance):
    devices = range(lax.axis_size(axis))
    route = [(i - distance, i) for i in devices if i - distance in devices]
    return lax.ppermute(block, axis, route)


def filled_up(lines, peers):
    spare = -len(lines) % peers
    return jnp.pad(lines, [(0, spare)] + [(0, 0)] * (lines.ndim - 1))


def in_order(parts, dim):
    lengths = list(parts.shape[1:])
    lengths[dim] *= parts.shape[0]
    return jnp.moveaxis(parts, 0, dim).reshape(lengths)


def from_everyone(array, axis):
    copies = jnp.broadcast_to(array, (lax.axis_size(axis), *array.shape))
    return lax.all_to_all(copies, axis, split_axis=0, concat_axis=0, tiled=True)


def gathered_copies(array, axis, dim):
    return in_order(from_everyone(array, axis), dim)


def in_blocks(array, dim, peers):
    lengths = array.shape
    parts = array.reshape(*lengths[:dim], peers, lengths[dim] // peers, *lengths[dim + 1 :])
    return jnp.moveaxis(parts, dim, 0)


def sent_and_summed(array, axis, dim):
    peers = lax.axis_size(axis)
    parts = lax.all_to_all(in_blocks(array, dim, peers), axis, 0, 0, tiled=True)
    return jnp.sum(parts, axis=0)


def total_of(array, axes):
    padded = filled_up(array, lax.axis_size(axes))
    whole = gathered_copies(sent_and_summed(padded, axes, 0), axes, 0)
    return lax.slice_in_dim(whole, 0, len(array)).reshape(array.shape)


def together(arrays, axis):
    flat, at, gathered = (jnp.concatenate([a.reshape(-1) for a in arrays]), 0, [])
    so_far = total_of(flat, axis)
    for a in arrays:
        gathered.append(so_far[at : at + a.size].reshape(a.shape))
        at += a.size
    return tuple(gathered)


def side_by_side(arrays, axis, dim, along):
    ends, at = ([], 0)
    for a in arrays[:-1]:
        at += a.shape[along]
        ends.append(at)
    both = jnp.concatenate(arrays, axis=along)
    return tuple(jnp.split(sent_and_summed(both, axis, dim), ends, axis=along))


def silu_slope(values):
    logistic = jax.nn.sigmoid(values)
    return logistic * (1.0 + values * (1.0 - logistic))


def tap_shift(values, row_step, col_step, image_side):
    pixels = values.shape[0]
    offset = row_step * image_side + col_step
    padded = jnp.pad(values, ((image_side + 1, image_side + 1), (0, 0)))
    moved = lax.slice_in_dim(
        padded, image_side + 1 + offset, image_side + 1 + offset + pixels, axis=0
    )
    column = lax.broadcasted_iota(jnp.int32, (pixels, 1), 0) % image_side + col_step
    inside = jnp.logical_and(column >= 0, column < image_side)
    return jnp.where(inside, moved, jnp.zeros_like(moved))


def inner_rows(left_operand, right_operand):
    return lax.dot_general(
        left_operand, right_operand, (((0,), (0,)), ((), ())), preferred_element_type=jnp.float32
    )


def inner_cols(left_operand, right_operand, accuracy=None):
    return lax.dot_general(
        left_operand,
        right_operand,
        (((1,), (1,)), ((), ())),
        precision=accuracy,
        preferred_element_type=jnp.float32,
    )


def block_backward(inputs, upstream, reduce_weight, spatial_weight, expand_weight, image_side):
    channels = reduce_weight.shape[1]
    pre_reduce = jnp.dot(inputs, reduce_weight, preferred_element_type=jnp.float32)
    hidden_one = jax.nn.silu(pre_reduce).astype(jnp.bfloat16)
    shifted = []
    pre_spatial = jnp.zeros((inputs.shape[0], channels), jnp.float32)
    for tap in range(9):
        moved = tap_shift(hidden_one, tap // 3 - 1, tap % 3 - 1, image_side)
        shifted.append(moved)
        pre_spatial = pre_spatial + jnp.dot(
            moved,
            spatial_weight[tap * channels : (tap + 1) * channels],
            preferred_element_type=jnp.float32,
        )
    hidden_two = jax.nn.silu(pre_spatial).astype(jnp.bfloat16)
    back_two = inner_cols(upstream, expand_weight)
    back_spatial = (back_two * silu_slope(pre_spatial)).astype(jnp.bfloat16)
    back_one = jnp.zeros((inputs.shape[0], channels), jnp.float32)
    for tap in range(9):
        tap_term = inner_cols(back_spatial, spatial_weight[tap * channels : (tap + 1) * channels])
        back_one = back_one + tap_shift(tap_term, 1 - tap // 3, 1 - tap % 3, image_side)
    back_reduce = (back_one * silu_slope(pre_reduce)).astype(jnp.bfloat16)
    leaving = (upstream.astype(jnp.float32) + inner_cols(back_reduce, reduce_weight)).astype(
        jnp.bfloat16
    )
    spatial_grad = jnp.concatenate(
        [inner_rows(shifted[tap], back_spatial) for tap in range(9)], axis=0
    )
    gradients = (inner_rows(inputs, back_reduce), spatial_grad, inner_rows(hidden_two, upstream))
    return (leaving, gradients)


def local(
    section_inputs,
    grad_in,
    loss_grad,
    w_reduce,
    w_spatial,
    w_expand,
    err_reduce,
    err_spatial,
    err_expand,
    prior_reduce,
    prior_spatial,
    prior_expand,
):
    image_side = SIDE
    weights = (w_reduce[0], w_spatial[0], w_expand[0])
    last_section = lax.axis_index("section") == lax.axis_size("section") - 1
    upstream = grad_in[0, 0]
    leaving = upstream
    totals = tuple((jnp.zeros(weights[member].shape, jnp.float32) for member in range(3)))
    for tick_index in range(section_inputs.shape[2]):
        if tick_index > 0:
            arrived = shifted_2(leaving, "section", -1)
            upstream = jnp.where(last_section, loss_grad[0, tick_index - 1], arrived)
        leaving, gradients = block_backward(
            section_inputs[0, 0, tick_index],
            upstream,
            weights[0],
            weights[1],
            weights[2],
            image_side,
        )
        totals = tuple((totals[member] + gradients[member] for member in range(3)))
    errors = (err_reduce[0, 0], err_spatial[0, 0], err_expand[0, 0])
    matrices = tuple((totals[member] + errors[member].astype(jnp.float32) for member in range(3)))
    priors = (prior_reduce[0], prior_spatial[0], prior_expand[0])
    factors = tuple((inner_cols(priors[member], matrices[member], precise) for member in range(3)))
    replicas = lax.axis_size(("node", "local"))
    replica_index = lax.axis_index(("node", "local"))
    basis_list = []
    summed = together((factors[0], factors[1], factors[2]), ("node", "local"))
    partial_rights = []
    for member in range(3):
        triangle = jnp.linalg.cholesky(inner_cols(summed[member], summed[member], precise))
        orthonormal = lax.linalg.triangular_solve(
            triangle, summed[member], left_side=True, lower=True
        )
        slice_width = orthonormal.shape[1] // replicas
        own_rows = lax.dynamic_slice_in_dim(
            orthonormal, replica_index * slice_width, slice_width, 1
        )
        basis_list.append(math.sqrt(orthonormal.shape[1]) * own_rows)
        partial_rights.append(
            jnp.dot(
                orthonormal, matrices[member], precision=precise, preferred_element_type=jnp.float32
            )
        )
    rights = (
        *side_by_side((partial_rights[0], partial_rights[1]), ("node", "local"), 1, 0),
        sent_and_summed(partial_rights[2], ("node", "local"), 1),
    )
    right_list = tuple(
        (rights[member] / (replicas * math.sqrt(matrices[member].shape[0])) for member in range(3))
    )
    return (
        leaving[None, None],
        basis_list[0][None],
        basis_list[1][None],
        basis_list[2][None],
        right_list[0][None],
        right_list[1][None],
        right_list[2][None],
    )


def solution(mesh):
    return jax.shard_map(
        local,
        mesh=mesh,
        in_specs=(
            P("section", ("node", "local"), None, None, None),
            P("section", ("node", "local"), None, None),
            P(("node", "local"), None, None, None),
            P("section", None, None),
            P("section", None, None),
            P("section", None, None),
            P("section", ("node", "local"), None, None),
            P("section", ("node", "local"), None, None),
            P("section", ("node", "local"), None, None),
            P("section", None, None),
            P("section", None, None),
            P("section", None, None),
        ),
        out_specs=(
            P("section", ("node", "local"), None, None),
            P("section", None, ("node", "local")),
            P("section", None, ("node", "local")),
            P("section", None, ("node", "local")),
            P("section", None, ("node", "local")),
            P("section", None, ("node", "local")),
            P("section", None, ("node", "local")),
        ),
        check_vma=False,
    )
```

profile of v0, /device:TPU:192, one launch (start us, length us, event | category | flops | bytes accessed | tf_op | source)
XLA Modules:
  0.0 210.0 jit_solution(16957765731569199983)
XLA Ops:
  0.7 4.9 %fusion.442 = (bf16[1,1,1,196,512]{4,2,3,1,0:T(2,128)(2,1)S(1)}, bf16[1,1,1,196,512]{4,2,3,1,0:T(2,128)(2,1)}, bf16[1,1,1,196,512]{4,2,3,1,0:T(2,128)(2,1)}, bf16[1,1,1,196,512]{4,2,3,1,0:T(2,128)(2,1)S(1)}) fusion(bf16[1,1,4,196,512]{4,2,3,1,0:T(4,128)(2,1)} %param.13), kind=kLoop, calls=%fused_computation.676 | loop fusion | bytes 1605632 | tf_op jit(solution)/shard_map/slice | solution.py:166
  11.4 1.9 collective-permute-start
  37.2 1.7 constant_dynamic-update-slice_fusion.6
  50.4 2.1 %collective-permute-start.1 = (bf16[196,512]{1,0:T(8,128)(2,1)S(1)}, bf16[196,512]{1,0:T(8,128)(2,1)S(1)}, u32[]{:S(2)}, u32[]{:S(2)}) collective-permute-start(bf16[196,512]{1,0:T(8,128)(2,1)S(1)} %add_convert_fusion.2), channel_id=1, source_target_pairs={{64,0},{128,64},{192,128},{256,192},{320,256},{384,320},{448,384},... | collective-permute-start | bytes 602120 | tf_op jit(solution)/shard_map/ppermute | solution.py:17
  65.6 6.2 %collective-permute-start.2 = (bf16[196,512]{1,0:T(8,128)(2,1)S(1)}, bf16[196,512]{1,0:T(8,128)(2,1)S(1)}, u32[]{:S(2)}, u32[]{:S(2)}) collective-permute-start(bf16[196,512]{1,0:T(8,128)(2,1)S(1)} %add_convert_fusion.1), channel_id=1, source_target_pairs={{64,0},{128,64},{192,128},{256,192},{320,256},{384,320},{448,384},... | collective-permute-start | bytes 602120 | tf_op jit(solution)/shard_map/ppermute | solution.py:17
  91.3 2.6 %convolution_bitcast_fusion = f32[32,2304]{1,0:T(8,128)S(1)} fusion(bf16[1,1,2304,256]{3,2,1,0:T(8,128)(2,1)S(1)} %copy-done.2, f32[1,1,2304,256]{3,2,1,0:T(8,128)S(1)} %get-tuple-element.73, f32[1,1,2304,256]{3,2,1,0:T(8,128)S(1)} %get-tuple-element.91, f32[1,1,2304,256]{3,2,1,0:T(8,128)S(1)} %copy-done.5, f32[1,1,2304,256]{3,2,1,0:T(8,128)S(1)} %get-tuple-element.127, ...), kind=kOutput, calls=%fused_computation | convolution fusion | flops 229441536 | bytes 10944512 | tf_op jit(solution)/shard_map/dot_general | solution.py:100
  94.7 9.1 %all-to-all-start = ((f32[64,1,1536]{2,1,0:T(1,128)}), f32[64,1,1536]{2,1,0:T(1,128)S(1)}, u32[]{:S(2)}, u32[]{:S(2)}) async-start(f32[64,1,1536]{2,1,0:T(1,128)} %bitcast.66), calls=%async_computation | async-start | bytes 786432 | tf_op jit(solution)/shard_map/all_to_all | solution.py:48
  107.8 1.7 constant_dynamic-update-slice_fusion.18
  112.9 1.7 constant_dynamic-update-slice_fusion.33
  114.6 4.5 %all-to-all-done = f32[64,1,1536]{2,1,0:T(1,128)S(1)} async-done(((f32[64,1,1536]{2,1,0:T(1,128)}), f32[64,1,1536]{2,1,0:T(1,128)S(1)}, u32[]{:S(2)}, u32[]{:S(2)}) %all-to-all-start) | async-done | bytes 393248 | tf_op jit(solution)/shard_map/all_to_all | solution.py:48
  120.3 6.0 %all-to-all-start.1 = ((f32[64,1,1536]{2,1,0:T(1,128)}), f32[64,1,1536]{2,1,0:T(1,128)}, u32[]{:S(2)}, u32[]{:S(2)}) async-start(f32[64,1,1536]{2,1,0:T(1,128)} %broadcast_in_dim.393), calls=%async_computation.1 | async-start | bytes 786432 | tf_op jit(solution)/shard_map/all_to_all | solution.py:33
  133.8 1.7 constant_dynamic-update-slice_fusion.27
  136.4 5.1 %all-to-all-done.1 = f32[64,1,1536]{2,1,0:T(1,128)} async-done(((f32[64,1,1536]{2,1,0:T(1,128)}), f32[64,1,1536]{2,1,0:T(1,128)}, u32[]{:S(2)}, u32[]{:S(2)}) %all-to-all-start.1) | async-done | bytes 393248 | tf_op jit(solution)/shard_map/all_to_all | solution.py:33
  141.6 2.0 reduce.5
  146.7 2.9 %cholesky.70 = f32[32,32]{1,0:T(8,128)S(1)} custom-call(f32[32,32]{1,0:T(8,128)S(1)} %fusion.331), custom_call_target="Cholesky" | custom-call | tf_op jit(solution)/shard_map/jit(cholesky)/cholesky | solution.py:184
  151.0 2.4 %custom-call.12 = f32[1,32,32]{1,2,0:T(8,128)S(1)} custom-call(f32[1,32,32]{2,1,0:T(8,128)S(1)} %fusion.325), custom_call_target="InvertDiagBlocksLowerTriangular" | custom-call | tf_op jit(solution)/shard_map/triangular_solve | solution.py:185
  156.1 2.9 %cholesky.81 = f32[32,32]{1,0:T(8,128)S(1)} custom-call(f32[32,32]{1,0:T(8,128)S(1)} %fusion.328), custom_call_target="Cholesky" | custom-call | tf_op jit(solution)/shard_map/jit(cholesky)/cholesky | solution.py:184
  160.4 2.4 %custom-call.13 = f32[1,32,32]{1,2,0:T(8,128)S(1)} custom-call(f32[1,32,32]{2,1,0:T(8,128)S(1)} %fusion.326), custom_call_target="InvertDiagBlocksLowerTriangular" | custom-call | tf_op jit(solution)/shard_map/triangular_solve | solution.py:185
  165.7 5.5 %all-to-all-start.3 = ((f32[64,1,256]{2,1,0:T(1,128)}), f32[64,1,256]{2,1,0:T(1,128)S(1)}, u32[]{:S(2)}, u32[]{:S(2)}) async-start(f32[64,1,256]{2,1,0:T(1,128)} %reshape.619), calls=%async_computation.3 | async-start | bytes 131072 | tf_op jit(solution)/shard_map/all_to_all | solution.py:48
  171.3 2.9 %cholesky.59 = f32[32,32]{1,0:T(8,128)S(1)} custom-call(f32[32,32]{1,0:T(8,128)S(1)} %fusion.333), custom_call_target="Cholesky" | custom-call | tf_op jit(solution)/shard_map/jit(cholesky)/cholesky | solution.py:184
  175.5 2.4 %custom-call.11 = f32[1,32,32]{1,2,0:T(8,128)S(1)} custom-call(f32[1,32,32]{2,1,0:T(8,128)S(1)} %fusion.324), custom_call_target="InvertDiagBlocksLowerTriangular" | custom-call | tf_op jit(solution)/shard_map/triangular_solve | solution.py:185
  179.7 5.4 %fusion.3 = f32[32,256]{1,0:T(8,128)S(1)} fusion(f32[32,2304]{1,0:T(8,128)S(1)} %fusion.329, bf16[1,1,2304,256]{3,2,1,0:T(8,128)(2,1)S(1)} %copy-done.2, f32[2304,256]{1,0:T(8,128)} %constant_dynamic-update-slice_fusion.27, f32[2304,256]{1,0:T(8,128)} %constant_dynamic-update-slice_fusion.18, f32[2304,256]{1,0:T(8,128)} %constant_dynamic-update-slice_fusion, ...), kind=kOutput, calls=%fused_computation.5 | convolution fusion | flops 229441536 | bytes 10944512 | tf_op jit(solution)/shard_map/dot_general | solution.py:194
  188.1 10.3 %all-to-all-start.2 = ((f32[64,1,256]{2,1,0:T(1,128)}), f32[64,1,256]{2,1,0:T(1,128)S(1)}, u32[]{:S(2)}, u32[]{:S(2)}) async-start(f32[64,1,256]{2,1,0:T(1,128)} %reshape.617), calls=%async_computation.2 | async-start | bytes 131072 | tf_op jit(solution)/shard_map/all_to_all | solution.py:48
  200.5 7.8 %all-to-all-done.2 = f32[64,1,256]{2,1,0:T(1,128)S(1)} async-done(((f32[64,1,256]{2,1,0:T(1,128)}), f32[64,1,256]{2,1,0:T(1,128)S(1)}, u32[]{:S(2)}, u32[]{:S(2)}) %all-to-all-start.2) | async-done | bytes 65568 | tf_op jit(solution)/shard_map/all_to_all | solution.py:48
  (291 shorter events, 111.6 us)
Async XLA Ops:
  0.6 5.0 %copy-start = (bf16[1,512,256]{2,1,0:T(8,128)(2,1)S(1)}, bf16[1,512,256]{2,1,0:T(8,128)(2,1)}, u32[]{:S(2)}) copy-start(bf16[1,512,256]{2,1,0:T(8,128)(2,1)} %param.16) | copy-start | bytes 786436
  0.6 5.2 %copy-start.1 = (bf16[1,2304,256]{2,1,0:T(8,128)(2,1)S(1)}, bf16[1,2304,256]{2,1,0:T(8,128)(2,1)}, u32[]{:S(2)}) copy-start(bf16[1,2304,256]{2,1,0:T(8,128)(2,1)} %param.17) | copy-start | bytes 3538948
  5.6 11.2 %copy-start.11 = (bf16[1,1,1,196,512]{4,2,3,1,0:T(2,128)(2,1)}, bf16[1,1,1,196,512]{4,2,3,1,0:T(2,128)(2,1)S(1)}, u32[]{:S(2)}) copy-start(bf16[1,1,1,196,512]{4,2,3,1,0:T(2,128)(2,1)S(1)} %get-tuple-element.43) | copy-start | bytes 602116
  11.4 34.9 %collective-permute-start = (bf16[196,512]{1,0:T(8,128)(2,1)}, bf16[196,512]{1,0:T(8,128)(2,1)}, u32[]{:S(2)}, u32[]{:S(2)}) collective-permute-start(bf16[196,512]{1,0:T(8,128)(2,1)} %fusion.15), channel_id=1, source_target_pairs={{64,0},{128,64},{192,128},{256,192},{320,256},{384,320},{448,384},... | collective-permute-start | bytes 602120 | tf_op jit(solution)/shard_map/ppermute | solution.py:17
  35.8 10.4 %copy-start.18 = (f32[196,256]{1,0:T(8,128)S(1)}, f32[196,256]{1,0:T(8,128)}, u32[]{:S(2)}) copy-start(f32[196,256]{1,0:T(8,128)} %convolution_add_fusion.23) | copy-start | bytes 602116
  36.5 7.5 %copy-start.9 = (f32[256,256]{1,0:T(8,128)S(1)}, f32[256,256]{1,0:T(8,128)}, u32[]{:S(2)}) copy-start(f32[256,256]{1,0:T(8,128)} %get-tuple-element.106) | copy-start | bytes 786436
  36.5 8.2 %copy-start.10 = (f32[256,256]{1,0:T(8,128)S(1)}, f32[256,256]{1,0:T(8,128)}, u32[]{:S(2)}) copy-start(f32[256,256]{1,0:T(8,128)} %get-tuple-element.108) | copy-start | bytes 786436
  36.5 9.9 %copy-start.21 = (bf16[1,3,196,512]{3,2,1,0:T(8,128)(2,1)S(1)}, bf16[1,3,196,512]{3,2,1,0:T(8,128)(2,1)}, u32[]{:S(2)}) copy-start(bf16[1,3,196,512]{3,2,1,0:T(8,128)(2,1)} %param.15) | copy-start | bytes 1806340
  37.2 10.1 %copy-start.30 = (bf16[1,256,512]{2,1,0:T(8,128)(2,1)S(1)}, bf16[1,256,512]{2,1,0:T(8,128)(2,1)}, u32[]{:S(2)}) copy-start(bf16[1,256,512]{2,1,0:T(8,128)(2,1)} %param.18) | copy-start | bytes 786436
  49.4 3.1 %copy-start.22 = (f32[256,512]{1,0:T(8,128)S(1)}, f32[256,512]{1,0:T(8,128)}, u32[]{:S(2)}) copy-start(f32[256,512]{1,0:T(8,128)} %fusion.120) | copy-start | bytes 1572868
  50.4 11.7 %collective-permute-start.1 = (bf16[196,512]{1,0:T(8,128)(2,1)S(1)}, bf16[196,512]{1,0:T(8,128)(2,1)S(1)}, u32[]{:S(2)}, u32[]{:S(2)}) collective-permute-start(bf16[196,512]{1,0:T(8,128)(2,1)S(1)} %add_convert_fusion.2), channel_id=1, source_target_pairs={{64,0},{128,64},{192,128},{256,192},{320,256},{384,320},{448,384},... | collective-permute-start | bytes 602120 | tf_op jit(solution)/shard_map/ppermute | solution.py:17
  55.4 6.5 %copy-start.16 = (bf16[1,1,1,196,512]{4,2,3,1,0:T(2,128)(2,1)S(1)}, bf16[1,1,1,196,512]{4,2,3,1,0:T(2,128)(2,1)}, u32[]{:S(2)}) copy-start(bf16[1,1,1,196,512]{4,2,3,1,0:T(2,128)(2,1)} %get-tuple-element.45) | copy-start | bytes 602116
  58.2 4.0 %copy-start.17 = (f32[196,256]{1,0:T(8,128)S(1)}, f32[196,256]{1,0:T(8,128)}, u32[]{:S(2)}) copy-start(f32[196,256]{1,0:T(8,128)} %convolution_add_fusion.14) | copy-start | bytes 602116
  65.6 12.1 %collective-permute-start.2 = (bf16[196,512]{1,0:T(8,128)(2,1)S(1)}, bf16[196,512]{1,0:T(8,128)(2,1)S(1)}, u32[]{:S(2)}, u32[]{:S(2)}) collective-permute-start(bf16[196,512]{1,0:T(8,128)(2,1)S(1)} %add_convert_fusion.1), channel_id=1, source_target_pairs={{64,0},{128,64},{192,128},{256,192},{320,256},{384,320},{448,384},... | collective-permute-start | bytes 602120 | tf_op jit(solution)/shard_map/ppermute | solution.py:17
  85.2 6.1 %copy-start.2 = (bf16[1,1,2304,256]{3,2,1,0:T(8,128)(2,1)S(1)}, bf16[1,1,2304,256]{3,2,1,0:T(8,128)(2,1)}, u32[]{:S(2)}) copy-start(bf16[1,1,2304,256]{3,2,1,0:T(8,128)(2,1)} %param.20) | copy-start | bytes 3538948
  85.2 6.1 %copy-start.5 = (f32[1,1,2304,256]{3,2,1,0:T(8,128)S(1)}, f32[1,1,2304,256]{3,2,1,0:T(8,128)}, u32[]{:S(2)}) copy-start(f32[1,1,2304,256]{3,2,1,0:T(8,128)} %copy-done.4) | copy-start | bytes 7077892
  85.2 6.1 %copy-start.27 = (f32[1,32,256]{2,1,0:T(8,128)S(1)}, f32[1,32,256]{2,1,0:T(8,128)}, u32[]{:S(2)}) copy-start(f32[1,32,256]{2,1,0:T(8,128)} %param.23) | copy-start | bytes 98308
  93.9 13.2 %copy-start.7 = (f32[256,256]{1,0:T(8,128)S(1)}, f32[256,256]{1,0:T(8,128)}, u32[]{:S(2)}) copy-start(f32[256,256]{1,0:T(8,128)} %get-tuple-element.90) | copy-start | bytes 786436
  94.7 24.4 %all-to-all-start = ((f32[64,1,1536]{2,1,0:T(1,128)}), f32[64,1,1536]{2,1,0:T(1,128)S(1)}, u32[]{:S(2)}, u32[]{:S(2)}) async-start(f32[64,1,1536]{2,1,0:T(1,128)} %bitcast.66), calls=%async_computation | async-start | bytes 786432 | tf_op jit(solution)/shard_map/all_to_all | solution.py:48
  107.8 20.2 %copy-start.8 = (f32[256,256]{1,0:T(8,128)S(1)}, f32[256,256]{1,0:T(8,128)}, u32[]{:S(2)}) copy-start(f32[256,256]{1,0:T(8,128)} %get-tuple-element.66) | copy-start | bytes 786436
  114.6 20.9 %copy-start.20 = (bf16[196,512]{1,0:T(8,128)(2,1)S(1)}, bf16[196,512]{1,0:T(8,128)(2,1)}, u32[]{:S(2)}) copy-start(bf16[196,512]{1,0:T(8,128)(2,1)} %copy-done.19) | copy-start | bytes 602116
  120.3 21.3 %all-to-all-start.1 = ((f32[64,1,1536]{2,1,0:T(1,128)}), f32[64,1,1536]{2,1,0:T(1,128)}, u32[]{:S(2)}, u32[]{:S(2)}) async-start(f32[64,1,1536]{2,1,0:T(1,128)} %broadcast_in_dim.393), calls=%async_computation.1 | async-start | bytes 786432 | tf_op jit(solution)/shard_map/all_to_all | solution.py:33
  165.7 22.4 %all-to-all-start.3 = ((f32[64,1,256]{2,1,0:T(1,128)}), f32[64,1,256]{2,1,0:T(1,128)S(1)}, u32[]{:S(2)}, u32[]{:S(2)}) async-start(f32[64,1,256]{2,1,0:T(1,128)} %reshape.619), calls=%async_computation.3 | async-start | bytes 131072 | tf_op jit(solution)/shard_map/all_to_all | solution.py:48
  188.1 20.2 %all-to-all-start.2 = ((f32[64,1,256]{2,1,0:T(1,128)}), f32[64,1,256]{2,1,0:T(1,128)S(1)}, u32[]{:S(2)}, u32[]{:S(2)}) async-start(f32[64,1,256]{2,1,0:T(1,128)} %reshape.617), calls=%async_computation.2 | async-start | bytes 131072 | tf_op jit(solution)/shard_map/all_to_all | solution.py:48
  (17 other events, 31.5 us)
where the time goes:
time: 211 us; the launch traced here: 210 us
  matrix products  69.2 us (33%)
  local copies, waits for them, and re-layouts  52.2 us (25%)
  starting transfers between devices  41.2 us (20%)
  other arithmetic  28 us (13%)
  waiting for transfers between devices  17.5 us (8%)
    unnamed x109, local copies, waits for them, and re-layouts  37.9 us
    dot_general x44, matrix products, inner_rows(): lax.dot_general(left_operand, right_operand, (((0,), (0,)), ((), ())), pr...  28.5 us
    all_to_all x3, starting transfers between devices, sent_and_summed(): parts = lax.all_to_all(in_blocks(array, dim, peers), axis, 0, 0, tiled=True)  24.9 us
    dot_general x50, matrix products, inner_cols(): lax.dot_general(left_operand, right_operand, (((1,), (1,)), ((), ())), pr...  18 us
    all_to_all x3, waiting for transfers between devices, sent_and_summed(): parts = lax.all_to_all(in_blocks(array, dim, peers), axis, 0, 0, tiled=True)  12.3 us
    another operation x9, other arithmetic, local(): jnp.linalg.cholesky(inner_cols(summed[member], summed[member], precise))  10.8 us
    ppermute x3, starting transfers between devices, shifted_2(): return lax.ppermute(block, axis, route)  10.2 us
    dot_general x36, matrix products, block_backward(): jnp.dot(moved, spatial_weight[tap * channels:(tap + 1) * channels], prefe...  10.2 us
  transfers between devices with their start and end apart: 7, of which 3 were waited for; matrix products, arithmetic and copies ran while one was open for 41% of the time, Pallas kernels for 0%

commit v1 on v0

v1 whole, which is shorter than its diff:
```python
import functools
import math

import jax
import jax.numpy as jnp
from jax import lax
from jax.experimental import pallas as pl
from jax.experimental.pallas import tpu as pltpu
from jax.sharding import PartitionSpec as P

SIDE = 14
PITCH = 16
ROWS = SIDE * PITCH
BLOCK = 256
PIXELS = SIDE * SIDE
TICKS = 4
OUT = 512
MID = 256
RANK = 32
TAPS = 9 * MID
COLUMNS = OUT + TAPS + MID
LANES = 128
TILED = COLUMNS // LANES * RANK
MESH = pl.DeviceIdType.MESH
F32 = jnp.float32
BF16 = jnp.bfloat16
PARTS = ((0, OUT), (OUT, TAPS), (OUT + TAPS, MID))


def dot(a, b):
    return jnp.dot(a, b, preferred_element_type=F32)


def dot_t(a, b):
    return lax.dot_general(a, b, (((1,), (1,)), ((), ())), preferred_element_type=F32)


def precise_dot_t(a, b):
    return lax.dot_general(
        a, b, (((1,), (1,)), ((), ())), preferred_element_type=F32, precision=lax.Precision.HIGHEST
    )


def precise_dot(a, b):
    return jnp.dot(a, b, preferred_element_type=F32, precision=lax.Precision.HIGHEST)


def two_terms(values):
    high = values.astype(BF16)
    low = (values - high.astype(F32)).astype(BF16)
    return jnp.concatenate([high, low], axis=0)


def folded(values):
    return values[:RANK] + values[RANK:]


def sigmoid(values):
    return 1.0 / (1.0 + jnp.exp(-values))


def spread_matrix():
    row = lax.broadcasted_iota(jnp.int32, (ROWS, PIXELS), 0)
    pixel = lax.broadcasted_iota(jnp.int32, (ROWS, PIXELS), 1)
    hit = ((row // PITCH) * SIDE + row % PITCH == pixel) & (row % PITCH < SIDE)
    return jnp.where(hit, 1.0, 0.0).astype(BF16)


def gather_matrix():
    row = lax.broadcasted_iota(jnp.int32, (PIXELS, ROWS), 1)
    pixel = lax.broadcasted_iota(jnp.int32, (PIXELS, ROWS), 0)
    hit = ((row // PITCH) * SIDE + row % PITCH == pixel) & (row % PITCH < SIDE)
    return jnp.where(hit, 1.0, 0.0).astype(BF16)


def shifted_copies(values, ref):
    ref[1, PITCH : PITCH + ROWS, :] = values.astype(BF16)
    ref[0, PITCH : PITCH + ROWS, :] = pltpu.roll(values, 1, 0).astype(BF16)
    ref[2, PITCH : PITCH + ROWS, :] = pltpu.roll(values, ROWS - 1, 0).astype(BF16)


def kernel(
    sizes,
    x_ref,
    grad_ref,
    loss_ref,
    wr_ref,
    ws_ref,
    we_ref,
    er_ref,
    es_ref,
    ee_ref,
    pr_ref,
    ps_ref,
    pe_ref,
    leaving_ref,
    basis_r_ref,
    basis_s_ref,
    basis_e_ref,
    right_r_ref,
    right_s_ref,
    right_e_ref,
    spread,
    x_all,
    cols,
    h2_all,
    ga_all,
    gb_all,
    up_all,
    shift,
    gshift,
    slope1,
    slope2,
    prior_rs,
    prior_e,
    acc,
    sent,
    arrived,
    tiled,
    core_in,
    half,
    y_in,
    x_in,
    full,
    pt2,
    right_tiles,
    right_tmp,
    rc_in,
    r2,
    rx_in,
    r3,
    ry_in,
    relay_send,
    relay_recv,
    core_send,
    core_recv,
    y_send,
    y_recv,
    x_send,
    x_recv,
    gy_send,
    gy_recv,
    gc_send,
    gc_recv,
    rc_send,
    rc_recv,
    rx_send,
    rx_recv,
    ry_send,
    ry_recv,
):
    sections, nodes, locals_ = sizes
    across = nodes // 2
    replicas = nodes * locals_
    section = lax.axis_index("section")
    node = lax.axis_index("node")
    local = lax.axis_index("local")
    core = lax.rem(node, 2)
    column = lax.div(node, 2)
    buddy = node + 1 - 2 * core
    share = TILED // 2 // locals_
    half_rows = TILED // 2
    e_rows = OUT // replicas
    r_rows = MID // replicas
    below = (lax.rem(section + sections - 1, sections), node, local)
    above = (lax.rem(section + 1, sections), node, local)

    def y_peer(d):
        return (section, node, lax.rem(local + d, locals_))

    def x_peer(d):
        return (section, lax.rem(column + d, across) * 2 + core, local)

    other_core = (section, buddy, local)

    barrier = pltpu.get_barrier_semaphore()
    pl.semaphore_signal(barrier, inc=1, device_id=above, device_id_type=MESH)
    pl.semaphore_signal(barrier, inc=1, device_id=other_core, device_id_type=MESH)
    for d in range(1, locals_):
        pl.semaphore_signal(barrier, inc=1, device_id=y_peer(d), device_id_type=MESH)
    for d in range(1, across):
        pl.semaphore_signal(barrier, inc=1, device_id=x_peer(d), device_id_type=MESH)

    def remote(src, dst, send, recv, device):
        return pltpu.make_async_remote_copy(
            src_ref=src, dst_ref=dst, send_sem=send, recv_sem=recv, device_id=device, device_id_type=MESH
        )

    spread[...] = spread_matrix()
    pad_rows = BLOCK - ROWS
    for t in range(TICKS):
        pad = pl.ds(t * BLOCK + ROWS, pad_rows)
        x_all[pad, :] = jnp.zeros((pad_rows, OUT), BF16)
        up_all[pad, :] = jnp.zeros((pad_rows, OUT), BF16)
        cols[pad, :] = jnp.zeros((pad_rows, TAPS), BF16)
        h2_all[pad, :] = jnp.zeros((pad_rows, MID), BF16)
        ga_all[pad, :] = jnp.zeros((pad_rows, MID), BF16)
        gb_all[pad, :] = jnp.zeros((pad_rows, MID), BF16)
    for b in range(3):
        for ref in (shift, gshift):
            ref[b, :PITCH, :] = jnp.zeros((PITCH, MID), BF16)
            ref[b, PITCH + ROWS :, :] = jnp.zeros((PITCH, MID), BF16)
    prior_rs[0] = two_terms(pr_ref[...])
    prior_rs[1] = two_terms(ps_ref[...])
    prior_e[...] = two_terms(pe_ref[...])

    def rows_of(t):
        return pl.ds(t * BLOCK, ROWS)

    def block_of(t):
        return pl.ds(t * BLOCK, BLOCK)

    def forward(t):
        x_all[rows_of(t), :] = dot(spread[...], x_ref[t]).astype(BF16)
        pre1 = dot(x_all[rows_of(t), :], wr_ref[...])
        q1 = sigmoid(pre1)
        pixel = lax.broadcasted_iota(jnp.int32, (ROWS, MID), 0) % PITCH < SIDE
        slope1[...] = jnp.where(pixel, q1 * (1.0 + pre1 * (1.0 - q1)), 0.0)
        shifted_copies(pre1 * q1, shift)
        for a in range(3):
            for b in range(3):
                at = (3 * a + b) * MID
                cols[rows_of(t), at : at + MID] = shift[b, a * PITCH : a * PITCH + ROWS, :]
        pre2 = dot(cols[rows_of(t), :], ws_ref[...])
        q2 = sigmoid(pre2)
        slope2[...] = q2 * (1.0 + pre2 * (1.0 - q2))
        h2_all[rows_of(t), :] = (pre2 * q2).astype(BF16)

    def backward(t):
        up = up_all[rows_of(t), :]
        gb = (dot_t(up, we_ref[...]) * slope2[...]).astype(BF16)
        gb_all[rows_of(t), :] = gb
        shifted_copies(gb.astype(F32), gshift)
        g1 = jnp.zeros((ROWS, MID), F32)
        for a in range(3):
            for b in range(3):
                at = (3 * a + b) * MID
                moved = gshift[2 - b, (2 - a) * PITCH : (2 - a) * PITCH + ROWS, :]
                g1 = g1 + dot_t(moved, ws_ref[at : at + MID, :])
        ga = (g1 * slope1[...]).astype(BF16)
        ga_all[rows_of(t), :] = ga
        return (up.astype(F32) + dot_t(ga, wr_ref[...])).astype(BF16)

    def left_terms(t):
        a_r = two_terms(folded(dot_t(prior_rs[0], ga_all[block_of(t), :])))
        acc[:, :OUT] += dot(a_r, x_all[block_of(t), :])
        a_s = two_terms(folded(dot_t(prior_rs[1], gb_all[block_of(t), :])))
        acc[:, OUT : OUT + TAPS] += dot(a_s, cols[block_of(t), :])
        a_e = two_terms(folded(dot_t(prior_e[...], up_all[block_of(t), :])))
        acc[:, OUT + TAPS :] += dot(a_e, h2_all[block_of(t), :])

    relay = [
        remote(sent.at[t], arrived.at[t], relay_send.at[t], relay_recv.at[t], below)
        for t in range(TICKS - 1)
    ]

    forward(0)
    up_all[rows_of(0), :] = dot(spread[...], grad_ref[...]).astype(BF16)
    for t in range(TICKS):
        if t > 0:
            lossy = dot(spread[...], loss_ref[t - 1]).astype(BF16)
            relay[t - 1].wait_recv()
            last = jnp.full((ROWS, OUT), section, jnp.int32) == sections - 1
            up_all[rows_of(t), :] = jnp.where(last, lossy, arrived[t - 1])
        dx = backward(t)
        if t < TICKS - 1:
            sent[t] = dx
            if t == 0:
                pl.semaphore_wait(barrier, locals_ + across)
            relay[t].start()
            if t == 0:
                acc[:, :OUT] = dot_t(prior_rs[0], er_ref[...])
                acc[:, OUT : OUT + TAPS] = dot_t(prior_rs[1], es_ref[...])
                acc[:, OUT + TAPS :] = dot_t(prior_e[...], ee_ref[...])
            left_terms(t)
            forward(t + 1)
    left_terms(TICKS - 1)

    for j in range(COLUMNS // LANES):
        tiled[j * RANK : (j + 1) * RANK, :] = (
            acc[:RANK, j * LANES : (j + 1) * LANES] + acc[RANK:, j * LANES : (j + 1) * LANES]
        )

    mine = pl.ds(pl.multiple_of(core * half_rows, half_rows), half_rows)
    theirs = pl.ds(pl.multiple_of((1 - core) * half_rows, half_rows), half_rows)
    to_core = remote(tiled.at[theirs], core_in, core_send, core_recv, other_core)
    to_core.start()
    leaving_ref[...] = dot(gather_matrix(), dx).astype(BF16)
    to_core.wait_recv()
    half[...] = tiled[mine, :] + core_in[...]
    to_y = []
    for d in range(1, locals_):
        at = pl.multiple_of(lax.rem(local + d, locals_) * share, share)
        to_y.append(
            remote(half.at[pl.ds(at, share)], y_in.at[d - 1], y_send.at[d - 1], y_recv.at[d - 1], y_peer(d))
        )
        to_y[-1].start()
    for copy in to_y:
        copy.wait_recv()
    summed = half[pl.ds(pl.multiple_of(local * share, share), share), :]
    for d in range(locals_ - 1):
        summed = summed + y_in[d]
    own = pl.ds(pl.multiple_of(core * half_rows + local * share, share), share)
    x_own = x_in.at[0]
    x_own[...] = summed
    to_x = []
    for d in range(1, across):
        to_x.append(remote(x_own, x_in.at[d], x_send.at[d - 1], x_recv.at[d - 1], x_peer(d)))
        to_x[-1].start()
    for copy in to_x:
        copy.wait_recv()
    for d in range(1, across):
        summed = summed + x_in[d]
    full[own, :] = summed
    from_y = []
    for d in range(1, locals_):
        from_y.append(remote(full.at[own], full.at[own], gy_send.at[d - 1], gy_recv.at[d - 1], y_peer(d)))
        from_y[-1].start()
    for copy in from_y:
        copy.wait_recv()
    from_core = remote(full.at[mine], full.at[mine], gc_send, gc_recv, other_core)
    from_core.start()
    from_core.wait_recv()

    for j in range(COLUMNS // LANES):
        values = full[j * RANK : (j + 1) * RANK, :]
        high = values.astype(BF16)
        pt2[:RANK, j * LANES : (j + 1) * LANES] = high
        pt2[RANK:, j * LANES : (j + 1) * LANES] = (values - high.astype(F32)).astype(BF16)
    b_r = two_terms(folded(dot_t(pt2[:, :OUT], x_all[...])))
    sum_r = folded(dot(b_r, ga_all[...]) + dot(pt2[:, :OUT], er_ref[...]))
    b_s = two_terms(folded(dot_t(pt2[:, OUT : OUT + TAPS], cols[...])))
    sum_s = folded(dot(b_s, gb_all[...]) + dot(pt2[:, OUT : OUT + TAPS], es_ref[...]))
    b_e = two_terms(folded(dot_t(pt2[:, OUT + TAPS :], h2_all[...])))
    sum_e = folded(dot(b_e, up_all[...]) + dot(pt2[:, OUT + TAPS :], ee_ref[...]))
    right_tiles[...] = jnp.concatenate([sum_e, jnp.zeros((LANES - RANK, OUT), F32)], axis=0).T
    zero = jnp.zeros((RANK, MID), F32)
    right_tmp[...] = jnp.concatenate([zero, sum_r, sum_s, zero], axis=0).T
    for i in range(r_rows):
        right_tiles[pl.ds(i, replicas, stride=e_rows), :] += right_tmp[pl.ds(i, replicas, stride=r_rows), :]

    group = locals_ * e_rows

    def group_at(column_, core_):
        return pl.ds(pl.multiple_of((column_ * 2 + core_) * group, group), group)

    to_core2 = []
    for i in range(across):
        to_core2.append(
            remote(right_tiles.at[group_at(i, 1 - core)], rc_in.at[i], rc_send.at[i], rc_recv.at[i], other_core)
        )
        to_core2[-1].start()

    def gram(start, width):
        terms = pt2[:, start : start + width]
        products = dot_t(terms, terms)
        return (products[:RANK, :RANK] + products[RANK:, :RANK]) + (products[:RANK, RANK:] + products[RANK:, RANK:])

    row_id = lax.broadcasted_iota(jnp.int32, (RANK, RANK), 0)
    col_id = lax.broadcasted_iota(jnp.int32, (RANK, RANK), 1)
    left = [gram(*part) for part in PARTS]
    inverse = [jnp.where(row_id == col_id, 1.0, 0.0) for _ in PARTS]

    def eliminate(steps):
        for k in steps:
            for m in range(3):
                factor = left[m][:, k : k + 1] * (1.0 / left[m][k : k + 1, k : k + 1])
                factor = jnp.where(row_id[:, :1] > k, factor, 0.0)
                row_left, row_inverse = left[m][k : k + 1, :], inverse[m][k : k + 1, :]
                left[m] = left[m] - factor * row_left
                inverse[m] = inverse[m] - factor * row_inverse

    for copy in to_core2:
        copy.wait_recv()
    for i in range(across):
        r2[i] = right_tiles[group_at(i, core), :] + rc_in[i]
    to_x2 = []
    for d in range(1, across):
        to_x2.append(
            remote(r2.at[lax.rem(column + d, across)], rx_in.at[d - 1], rx_send.at[d - 1], rx_recv.at[d - 1], x_peer(d))
        )
        to_x2[-1].start()
    eliminate(range(RANK // 2))
    for copy in to_x2:
        copy.wait_recv()
    total = r2[column]
    for d in range(across - 1):
        total = total + rx_in[d]
    r3[...] = total
    to_y2 = []
    for d in range(1, locals_):
        at = pl.multiple_of(lax.rem(local + d, locals_) * e_rows, e_rows)
        to_y2.append(
            remote(r3.at[pl.ds(at, e_rows)], ry_in.at[d - 1], ry_send.at[d - 1], ry_recv.at[d - 1], y_peer(d))
        )
        to_y2[-1].start()
    eliminate(range(RANK // 2, RANK))
    for m in range(3):
        pivots = jnp.sum(jnp.where(row_id == col_id, left[m], 0.0), axis=1, keepdims=True)
        inverse[m] = inverse[m] * lax.rsqrt(pivots)

    replica = node * locals_ + local
    for m, ref in enumerate((basis_r_ref, basis_s_ref, basis_e_ref)):
        start, rows = PARTS[m]
        width = rows // replicas
        at = start + replica * width
        first = at // LANES
        tiles = 1 if LANES % width == 0 else width // LANES + 2
        pieces = []
        for i in range(tiles):
            j = jnp.minimum(first + i, COLUMNS // LANES - 1)
            pieces.append(full[pl.ds(pl.multiple_of(j * RANK, RANK), RANK), :])
        window = pieces[0] if tiles == 1 else jnp.concatenate(pieces, axis=1)
        span = tiles * LANES
        window = pltpu.roll(window, lax.rem(span - (at - first * LANES), span), 1)
        if m == 1:
            ref[...] = precise_dot(inverse[m], window)[:, :width] * math.sqrt(rows)
        else:
            ref[...] = precise_dot_t(window.T[:width, :], inverse[m]) * math.sqrt(rows)

    for copy in to_y2:
        copy.wait_recv()
    total = r3[pl.ds(pl.multiple_of(local * e_rows, e_rows), e_rows), :]
    for d in range(locals_ - 1):
        total = total + ry_in[d]
    right_e_ref[...] = precise_dot_t(total[:, :RANK], inverse[2]) / (replicas * math.sqrt(MID))
    few = total[:, RANK : 2 * RANK]
    right_r_ref[...] = precise_dot_t(few, inverse[0])[:r_rows, :] / (replicas * math.sqrt(OUT))
    few = total[:, 2 * RANK : 3 * RANK]
    right_s_ref[...] = precise_dot_t(few, inverse[1])[:r_rows, :] / (replicas * math.sqrt(TAPS))

    for copy in (*relay, to_core, *to_y, *to_x, *from_y, from_core, *to_core2, *to_x2, *to_y2):
        copy.wait_send()


def on_device(
    sizes,
    section_inputs,
    grad_in,
    loss_grad,
    w_reduce,
    w_spatial,
    w_expand,
    err_reduce,
    err_spatial,
    err_expand,
    prior_reduce,
    prior_spatial,
    prior_expand,
):
    sections, nodes, locals_ = sizes
    across = nodes // 2
    replicas = nodes * locals_
    share = TILED // 2 // locals_
    e_rows = OUT // replicas
    r_rows = MID // replicas
    group = locals_ * e_rows
    vmem = pl.BlockSpec(memory_space=pltpu.VMEM)
    dma = pltpu.SemaphoreType.DMA
    more = max(across - 1, 1)
    scratch = [
        pltpu.VMEM((ROWS, PIXELS), BF16),
        pltpu.VMEM((TICKS * BLOCK, OUT), BF16),
        pltpu.VMEM((TICKS * BLOCK, TAPS), BF16),
        pltpu.VMEM((TICKS * BLOCK, MID), BF16),
        pltpu.VMEM((TICKS * BLOCK, MID), BF16),
        pltpu.VMEM((TICKS * BLOCK, MID), BF16),
        pltpu.VMEM((TICKS * BLOCK, OUT), BF16),
        pltpu.VMEM((3, ROWS + 2 * PITCH, MID), BF16),
        pltpu.VMEM((3, ROWS + 2 * PITCH, MID), BF16),
        pltpu.VMEM((ROWS, MID), F32),
        pltpu.VMEM((ROWS, MID), F32),
        pltpu.VMEM((2, 2 * RANK, MID), BF16),
        pltpu.VMEM((2 * RANK, OUT), BF16),
        pltpu.VMEM((2 * RANK, COLUMNS), F32),
        pltpu.VMEM((TICKS - 1, ROWS, OUT), BF16),
        pltpu.VMEM((TICKS - 1, ROWS, OUT), BF16),
        pltpu.VMEM((TILED, LANES), F32),
        pltpu.VMEM((TILED // 2, LANES), F32),
        pltpu.VMEM((TILED // 2, LANES), F32),
        pltpu.VMEM((locals_ - 1, share, LANES), F32),
        pltpu.VMEM((across, share, LANES), F32),
        pltpu.VMEM((TILED, LANES), F32),
        pltpu.VMEM((2 * RANK, COLUMNS), BF16),
        pltpu.VMEM((OUT, LANES), F32),
        pltpu.VMEM((MID, LANES), F32),
        pltpu.VMEM((across, group, LANES), F32),
        pltpu.VMEM((across, group, LANES), F32),
        pltpu.VMEM((more, group, LANES), F32),
        pltpu.VMEM((group, LANES), F32),
        pltpu.VMEM((locals_ - 1, e_rows, LANES), F32),
        dma((TICKS - 1,)),
        dma((TICKS - 1,)),
        dma,
        dma,
        dma((locals_ - 1,)),
        dma((locals_ - 1,)),
        dma((more,)),
        dma((more,)),
        dma((locals_ - 1,)),
        dma((locals_ - 1,)),
        dma,
        dma,
        dma((across,)),
        dma((across,)),
        dma((more,)),
        dma((more,)),
        dma((locals_ - 1,)),
        dma((locals_ - 1,)),
    ]
    shapes = (
        jax.ShapeDtypeStruct((PIXELS, OUT), BF16),
        jax.ShapeDtypeStruct((OUT // replicas, RANK), F32),
        jax.ShapeDtypeStruct((RANK, TAPS // replicas), F32),
        jax.ShapeDtypeStruct((MID // replicas, RANK), F32),
        jax.ShapeDtypeStruct((r_rows, RANK), F32),
        jax.ShapeDtypeStruct((r_rows, RANK), F32),
        jax.ShapeDtypeStruct((e_rows, RANK), F32),
    )
    results = pl.pallas_call(
        functools.partial(kernel, sizes),
        out_shape=shapes,
        in_specs=[vmem] * 12,
        out_specs=(vmem,) * 7,
        scratch_shapes=scratch,
        compiler_params=pltpu.CompilerParams(
            collective_id=0, has_side_effects=True, vmem_limit_bytes=56 * 1024 * 1024
        ),
        cost_estimate=pl.CostEstimate(flops=5_000_000_000, bytes_accessed=6_000_000, transcendentals=500_000),
    )(
        section_inputs[0, 0],
        grad_in[0, 0],
        loss_grad[0],
        w_reduce[0],
        w_spatial[0],
        w_expand[0],
        err_reduce[0, 0],
        err_spatial[0, 0],
        err_expand[0, 0],
        prior_reduce[0],
        prior_spatial[0],
        prior_expand[0],
    )
    leaving, basis_r, basis_s, *others = results
    return (leaving[None, None], basis_r.T[None], basis_s[None], *(other.T[None] for other in others))


def solution(mesh):
    sizes = (mesh.shape["section"], mesh.shape["node"], mesh.shape["local"])
    replicas = ("node", "local")
    return jax.shard_map(
        functools.partial(on_device, sizes),
        mesh=mesh,
        in_specs=(
            P("section", replicas),
            P("section", replicas),
            P(replicas),
            P("section"),
            P("section"),
            P("section"),
            P("section", replicas),
            P("section", replicas),
            P("section", replicas),
            P("section"),
            P("section"),
            P("section"),
        ),
        out_specs=(
            P("section", replicas),
            P("section", None, replicas),
            P("section", None, replicas),
            P("section", None, replicas),
            P("section", None, replicas),
            P("section", None, replicas),
            P("section", None, replicas),
        ),
        check_vma=False,
    )
```

time: 211 us -> 87.2 us (0.41)
  the two profiles are of different devices: /device:TPU:192 before, /device:TPU:64 now
where the time goes in v1:
time: 87.2 us; the launch traced here: 86.8 us
  Pallas kernels  74.7 us (86%)
  local copies, waits for them, and re-layouts  11.4 us (13%)
    pallas_call x1, Pallas kernels, on_device(): pl.pallas_call(functools.partial(kernel, sizes), out_shape=shapes, in_spe...  74.7 us
    unnamed x8, local copies, waits for them, and re-layouts  11.4 us

profile of v1, /device:TPU:64, one launch (start us, length us, event | category | flops | bytes accessed | tf_op | source)
XLA Modules:
  0.0 86.8 jit_solution(6837180638435800070)
XLA Ops:
  0.6 2.2 %copy.21 = bf16[1,1,4,196,512]{4,3,2,1,0:T(8,128)(2,1)} copy(bf16[1,1,4,196,512]{4,2,3,1,0:T(4,128)(2,1)} %param.12) | data formatting | bytes 1605632 | tf_op args[0]
  2.8 74.7 %shard_map.171 = (bf16[196,512]{1,0:T(8,128)(2,1)}, f32[8,32]{1,0:T(8,128)}, f32[32,36]{1,0:T(8,128)}, f32[4,32]{1,0:T(4,128)}, f32[4,32]{1,0:T(4,128)}, /*index=5*/f32[4,32]{1,0:T(4,128)}, f32[8,32]{1,0:T(8,128)}) custom-call(bf16[4,196,512]{2,1,0:T(8,128)(2,1)} %bitcast.31, bf16[196,512]{1,0:T(8,128)(2,1)} %bitcast.46, bf16[3,196,512]{2,1,0:T(8,128)(2,1)} %bitcast.41, ...), custom_call_target="tpu_custom_call" | custom-call | flops 5000000000 | bytes 6000000 | tf_op jit(solution)/shard_map/pallas_call | solution.py:520
  77.6 1.6 %copy.29 = bf16[1,1,196,512]{3,2,1,0:T(8,128)(2,1)} copy(bf16[1,1,196,512]{3,2,1,0:T(8,128)(2,1)} %bitcast.32) | data formatting | bytes 401408
  79.2 1.3 %copy.30 = f32[1,32,8]{1,2,0:T(8,128)} copy(f32[1,32,8]{1,2,0:T(8,128)} %bitcast.35) | data formatting | bytes 2048
  80.5 1.3 %copy.31 = f32[1,32,36]{2,1,0:T(8,128)} copy(f32[1,32,36]{2,1,0:T(8,128)} %bitcast.33) | data formatting | bytes 9216
  81.8 1.2 %copy.32 = f32[1,32,4]{1,2,0:T(4,128)} copy(f32[1,32,4]{1,2,0:T(4,128)} %bitcast.38) | data formatting | bytes 1024
  83.0 1.3 %copy.33 = f32[1,32,4]{1,2,0:T(4,128)} copy(f32[1,32,4]{1,2,0:T(4,128)} %bitcast.37) | data formatting | bytes 1024
  84.3 1.3 %copy.34 = f32[1,32,4]{1,2,0:T(4,128)} copy(f32[1,32,4]{1,2,0:T(4,128)} %bitcast.36) | data formatting | bytes 1024
  85.5 1.3 %copy.35 = f32[1,32,8]{1,2,0:T(8,128)} copy(f32[1,32,8]{1,2,0:T(8,128)} %bitcast.34) | data formatting | bytes 2048

commit v2 on v1

--- a/solution.py
+++ b/solution.py
@@ -18,6 +18,8 @@
 MID = 256
 RANK = 32
 TAPS = 9 * MID
+CUTS = (0, 6, 10)
+PIECES = len(CUTS)
 COLUMNS = OUT + TAPS + MID
 LANES = 128
 TILED = COLUMNS // LANES * RANK
@@ -100,6 +102,15 @@
     right_r_ref,
     right_s_ref,
     right_e_ref,
+    x,
+    grad,
+    loss,
+    wr,
+    ws,
+    we,
+    er,
+    es,
+    ee,
     spread,
     x_all,
     cols,
@@ -107,6 +118,10 @@
     ga_all,
     gb_all,
     up_all,
+    ws_t,
+    wr_t,
+    we_t,
+    gcols,
     shift,
     gshift,
     slope1,
@@ -119,10 +134,11 @@
     tiled,
     core_in,
     half,
+    half_out,
     y_in,
     x_in,
     full,
-    pt2,
+    pt,
     right_tiles,
     right_tmp,
     rc_in,
@@ -130,6 +146,7 @@
     rx_in,
     r3,
     ry_in,
+    load_sem,
     relay_send,
     relay_recv,
     core_send,
@@ -173,6 +190,21 @@
 
     other_core = (section, buddy, local)
 
+    pairs = (
+        (x_ref.at[0], x.at[0]),
+        (wr_ref, wr),
+        (ws_ref, ws),
+        (grad_ref, grad),
+        (we_ref, we),
+        *((x_ref.at[t], x.at[t]) for t in range(1, TICKS)),
+        (er_ref, er),
+        (es_ref, es),
+        (ee_ref, ee),
+        (loss_ref, loss),
+    )
+    loads = [pltpu.make_async_copy(a, b, load_sem.at[i]) for i, (a, b) in enumerate(pairs)]
+    for load in loads:
+        load.start()
     barrier = pltpu.get_barrier_semaphore()
     pl.semaphore_signal(barrier, inc=1, device_id=above, device_id_type=MESH)
     pl.semaphore_signal(barrier, inc=1, device_id=other_core, device_id_type=MESH)
@@ -210,36 +242,54 @@
     def block_of(t):
         return pl.ds(t * BLOCK, BLOCK)
 
-    def forward(t):
-        x_all[rows_of(t), :] = dot(spread[...], x_ref[t]).astype(BF16)
-        pre1 = dot(x_all[rows_of(t), :], wr_ref[...])
+    def forward_one(t):
+        x_all[rows_of(t), :] = dot(spread[...], x[t]).astype(BF16)
+        pre1 = dot(x_all[rows_of(t), :], wr[...])
         q1 = sigmoid(pre1)
         pixel = lax.broadcasted_iota(jnp.int32, (ROWS, MID), 0) % PITCH < SIDE
-        slope1[...] = jnp.where(pixel, q1 * (1.0 + pre1 * (1.0 - q1)), 0.0)
+        slope1[t % 2] = jnp.where(pixel, q1 * (1.0 + pre1 * (1.0 - q1)), 0.0)
         shifted_copies(pre1 * q1, shift)
         for a in range(3):
             for b in range(3):
                 at = (3 * a + b) * MID
                 cols[rows_of(t), at : at + MID] = shift[b, a * PITCH : a * PITCH + ROWS, :]
-        pre2 = dot(cols[rows_of(t), :], ws_ref[...])
+
+    def forward_two(t):
+        pre2 = dot(cols[rows_of(t), :], ws[...])
         q2 = sigmoid(pre2)
-        slope2[...] = q2 * (1.0 + pre2 * (1.0 - q2))
+        slope2[t % 2] = q2 * (1.0 + pre2 * (1.0 - q2))
         h2_all[rows_of(t), :] = (pre2 * q2).astype(BF16)
 
-    def backward(t):
-        up = up_all[rows_of(t), :]
-        gb = (dot_t(up, we_ref[...]) * slope2[...]).astype(BF16)
-        gb_all[rows_of(t), :] = gb
-        shifted_copies(gb.astype(F32), gshift)
-        g1 = jnp.zeros((ROWS, MID), F32)
+    def gb_rows(t, first, last):
+        count = (last - first) * PITCH
+        at = first * PITCH
+        rows = pl.ds(t * BLOCK + at, count)
+        if t > 0:
+            is_last = jnp.full((count, OUT), section, jnp.int32) == sections - 1
+            up_all[rows, :] = jnp.where(is_last, up_all[rows, :], arrived[t - 1, at : at + count, :])
+        gb = (dot(up_all[rows, :], we_t[...]) * slope2[t % 2, at : at + count, :]).astype(BF16)
+        gb_all[rows, :] = gb
+        gb = gb.astype(F32)
+        to = slice(PITCH + at, PITCH + at + count)
+        gshift[1, to, :] = gb.astype(BF16)
+        gshift[0, to, :] = pltpu.roll(gb, 1, 0).astype(BF16)
+        gshift[2, to, :] = pltpu.roll(gb, count - 1, 0).astype(BF16)
+
+    def ga_rows(t, first, last):
+        count = (last - first) * PITCH
+        at = first * PITCH
         for a in range(3):
             for b in range(3):
-                at = (3 * a + b) * MID
-                moved = gshift[2 - b, (2 - a) * PITCH : (2 - a) * PITCH + ROWS, :]
-                g1 = g1 + dot_t(moved, ws_ref[at : at + MID, :])
-        ga = (g1 * slope1[...]).astype(BF16)
-        ga_all[rows_of(t), :] = ga
-        return (up.astype(F32) + dot_t(ga, wr_ref[...])).astype(BF16)
+                tap = (3 * a + b) * MID
+                gcols[at : at + count, tap : tap + MID] = gshift[
+                    2 - b, (2 - a) * PITCH + at : (2 - a) * PITCH + at + count, :
+                ]
+        g1 = dot(gcols[at : at + count, :], ws_t[...])
+        ga_all[pl.ds(t * BLOCK + at, count), :] = (g1 * slope1[t % 2, at : at + count, :]).astype(BF16)
+
+    def dx_rows(t, first, last):
+        rows = pl.ds(t * BLOCK + first * PITCH, (last - first) * PITCH)
+        return (up_all[rows, :].astype(F32) + dot(ga_all[rows, :], wr_t[...])).astype(BF16)
 
     def left_terms(t):
         a_r = two_terms(folded(dot_t(prior_rs[0], ga_all[block_of(t), :])))
@@ -249,31 +299,65 @@
         a_e = two_terms(folded(dot_t(prior_e[...], up_all[block_of(t), :])))
         acc[:, OUT + TAPS :] += dot(a_e, h2_all[block_of(t), :])
 
-    relay = [
-        remote(sent.at[t], arrived.at[t], relay_send.at[t], relay_recv.at[t], below)
-        for t in range(TICKS - 1)
-    ]
-
-    forward(0)
-    up_all[rows_of(0), :] = dot(spread[...], grad_ref[...]).astype(BF16)
+    def piece(t, part):
+        first = CUTS[part] - t if part else 0
+        return first, CUTS[part + 1] - t if part < PIECES - 1 else SIDE
+
+    relay = {}
+    for t in range(TICKS - 1):
+        for part in range(PIECES):
+            first, last = piece(t, part)
+            rows = pl.ds(first * PITCH, (last - first) * PITCH)
+            sems = (relay_send.at[t, part], relay_recv.at[t, part])
+            relay[t, part] = remote(sent.at[t, rows], arrived.at[t, rows], *sems, below)
+
+    def arrive(count):
+        for load in loads[arrive.done : count]:
+            load.wait()
+        arrive.done = count
+
+    arrive.done = 0
+    arrive(2)
+    forward_one(0)
+    arrive(3)
+    forward_two(0)
+    for k in range(9):
+        ws_t[k * MID : (k + 1) * MID, :] = ws[k * MID : (k + 1) * MID, :].T
+    arrive(5)
+    we_t[...] = we[...].T
+    wr_t[...] = wr[...].T
+    up_all[rows_of(0), :] = dot(spread[...], grad[...]).astype(BF16)
+
+    def shadow(t, part):
+        if part == 0:
+            arrive(8)
+            forward_one(t + 1)
+        elif part == 1:
+            forward_two(t + 1)
+        else:
+            if t == 0:
+                arrive(12)
+                acc[:, :OUT] = dot_t(prior_rs[0], er[...])
+                acc[:, OUT : OUT + TAPS] = dot_t(prior_rs[1], es[...])
+                acc[:, OUT + TAPS :] = dot_t(prior_e[...], ee[...])
+            up_all[rows_of(t + 1), :] = dot(spread[...], loss[t]).astype(BF16)
+            left_terms(t)
+
     for t in range(TICKS):
-        if t > 0:
-            lossy = dot(spread[...], loss_ref[t - 1]).astype(BF16)
-            relay[t - 1].wait_recv()
-            last = jnp.full((ROWS, OUT), section, jnp.int32) == sections - 1
-            up_all[rows_of(t), :] = jnp.where(last, lossy, arrived[t - 1])
-        dx = backward(t)
-        if t < TICKS - 1:
-            sent[t] = dx
-            if t == 0:
-                pl.semaphore_wait(barrier, locals_ + across)
-            relay[t].start()
-            if t == 0:
-                acc[:, :OUT] = dot_t(prior_rs[0], er_ref[...])
-                acc[:, OUT : OUT + TAPS] = dot_t(prior_rs[1], es_ref[...])
-                acc[:, OUT + TAPS :] = dot_t(prior_e[...], ee_ref[...])
-            left_terms(t)
-            forward(t + 1)
+        for part in range(PIECES):
+            if t > 0:
+                relay[t - 1, part].wait_recv()
+                gb_rows(t, *piece(t - 1, part))
+            elif part == 0:
+                gb_rows(t, 0, SIDE)
+            ga_rows(t, *piece(t, part))
+            if t < TICKS - 1:
+                first, last = piece(t, part)
+                sent[t, first * PITCH : last * PITCH, :] = dx_rows(t, first, last)
+                if t == 0 and part == 0:
+                    pl.semaphore_wait(barrier, locals_ + across)
+                relay[t, part].start()
+                shadow(t, part)
     left_terms(TICKS - 1)
 
     for j in range(COLUMNS // LANES):
@@ -285,33 +369,35 @@
     theirs = pl.ds(pl.multiple_of((1 - core) * half_rows, half_rows), half_rows)
     to_core = remote(tiled.at[theirs], core_in, core_send, core_recv, other_core)
     to_core.start()
-    leaving_ref[...] = dot(gather_matrix(), dx).astype(BF16)
+    leaving_ref[...] = dot(gather_matrix(), dx_rows(TICKS - 1, 0, SIDE)).astype(BF16)
     to_core.wait_recv()
     half[...] = tiled[mine, :] + core_in[...]
+    half_out[...] = half[...].astype(BF16)
     to_y = []
     for d in range(1, locals_):
         at = pl.multiple_of(lax.rem(local + d, locals_) * share, share)
         to_y.append(
-            remote(half.at[pl.ds(at, share)], y_in.at[d - 1], y_send.at[d - 1], y_recv.at[d - 1], y_peer(d))
+            remote(half_out.at[pl.ds(at, share)], y_in.at[d - 1], y_send.at[d - 1], y_recv.at[d - 1], y_peer(d))
         )
         to_y[-1].start()
     for copy in to_y:
         copy.wait_recv()
     summed = half[pl.ds(pl.multiple_of(local * share, share), share), :]
     for d in range(locals_ - 1):
-        summed = summed + y_in[d]
+        summed = summed + y_in[d].astype(F32)
     own = pl.ds(pl.multiple_of(core * half_rows + local * share, share), share)
-    x_own = x_in.at[0]
+    x_own = x_in.at[column]
     x_own[...] = summed
     to_x = []
     for d in range(1, across):
-        to_x.append(remote(x_own, x_in.at[d], x_send.at[d - 1], x_recv.at[d - 1], x_peer(d)))
+        to_x.append(remote(x_own, x_own, x_send.at[d - 1], x_recv.at[d - 1], x_peer(d)))
         to_x[-1].start()
     for copy in to_x:
         copy.wait_recv()
+    summed = x_in[0]
     for d in range(1, across):
         summed = summed + x_in[d]
-    full[own, :] = summed
+    full[own, :] = summed.astype(BF16)
     from_y = []
     for d in range(1, locals_):
         from_y.append(remote(full.at[own], full.at[own], gy_send.at[d - 1], gy_recv.at[d - 1], y_peer(d)))
@@ -323,16 +409,13 @@
     from_core.wait_recv()
 
     for j in range(COLUMNS // LANES):
-        values = full[j * RANK : (j + 1) * RANK, :]
-        high = values.astype(BF16)
-        pt2[:RANK, j * LANES : (j + 1) * LANES] = high
-        pt2[RANK:, j * LANES : (j + 1) * LANES] = (values - high.astype(F32)).astype(BF16)
-    b_r = two_terms(folded(dot_t(pt2[:, :OUT], x_all[...])))
-    sum_r = folded(dot(b_r, ga_all[...]) + dot(pt2[:, :OUT], er_ref[...]))
-    b_s = two_terms(folded(dot_t(pt2[:, OUT : OUT + TAPS], cols[...])))
-    sum_s = folded(dot(b_s, gb_all[...]) + dot(pt2[:, OUT : OUT + TAPS], es_ref[...]))
-    b_e = two_terms(folded(dot_t(pt2[:, OUT + TAPS :], h2_all[...])))
-    sum_e = folded(dot(b_e, up_all[...]) + dot(pt2[:, OUT + TAPS :], ee_ref[...]))
+        pt[:, j * LANES : (j + 1) * LANES] = full[j * RANK : (j + 1) * RANK, :]
+    b_r = two_terms(dot_t(pt[:, :OUT], x_all[...]))
+    sum_r = folded(dot(b_r, ga_all[...])) + dot(pt[:, :OUT], er[...])
+    b_s = two_terms(dot_t(pt[:, OUT : OUT + TAPS], cols[...]))
+    sum_s = folded(dot(b_s, gb_all[...])) + dot(pt[:, OUT : OUT + TAPS], es[...])
+    b_e = two_terms(dot_t(pt[:, OUT + TAPS :], h2_all[...]))
+    sum_e = folded(dot(b_e, up_all[...])) + dot(pt[:, OUT + TAPS :], ee[...])
     right_tiles[...] = jnp.concatenate([sum_e, jnp.zeros((LANES - RANK, OUT), F32)], axis=0).T
     zero = jnp.zeros((RANK, MID), F32)
     right_tmp[...] = jnp.concatenate([zero, sum_r, sum_s, zero], axis=0).T
@@ -352,9 +435,8 @@
         to_core2[-1].start()
 
     def gram(start, width):
-        terms = pt2[:, start : start + width]
-        products = dot_t(terms, terms)
-        return (products[:RANK, :RANK] + products[RANK:, :RANK]) + (products[:RANK, RANK:] + products[RANK:, RANK:])
+        terms = pt[:, start : start + width]
+        return dot_t(terms, terms)
 
     row_id = lax.broadcasted_iota(jnp.int32, (RANK, RANK), 0)
     col_id = lax.broadcasted_iota(jnp.int32, (RANK, RANK), 1)
@@ -409,7 +491,7 @@
         pieces = []
         for i in range(tiles):
             j = jnp.minimum(first + i, COLUMNS // LANES - 1)
-            pieces.append(full[pl.ds(pl.multiple_of(j * RANK, RANK), RANK), :])
+            pieces.append(full[pl.ds(pl.multiple_of(j * RANK, RANK), RANK), :].astype(F32))
         window = pieces[0] if tiles == 1 else jnp.concatenate(pieces, axis=1)
         span = tiles * LANES
         window = pltpu.roll(window, lax.rem(span - (at - first * LANES), span), 1)
@@ -429,8 +511,13 @@
     few = total[:, 2 * RANK : 3 * RANK]
     right_s_ref[...] = precise_dot_t(few, inverse[1])[:r_rows, :] / (replicas * math.sqrt(TAPS))
 
-    for copy in (*relay, to_core, *to_y, *to_x, *from_y, from_core, *to_core2, *to_x2, *to_y2):
+    for copy in (*relay.values(), to_core, *to_y, *to_x, *from_y, from_core, *to_core2, *to_x2, *to_y2):
         copy.wait_send()
+
+
+def hand_over(*refs):
+    for source, target in zip(refs[:7], refs[7:]):
+        target[...] = source[...]
 
 
 def on_device(
@@ -458,7 +545,17 @@
     vmem = pl.BlockSpec(memory_space=pltpu.VMEM)
     dma = pltpu.SemaphoreType.DMA
     more = max(across - 1, 1)
+    hbm = pl.BlockSpec(memory_space=pltpu.HBM)
     scratch = [
+        pltpu.VMEM((TICKS, PIXELS, OUT), BF16),
+        pltpu.VMEM((PIXELS, OUT), BF16),
+        pltpu.VMEM((TICKS - 1, PIXELS, OUT), BF16),
+        pltpu.VMEM((OUT, MID), BF16),
+        pltpu.VMEM((TAPS, MID), BF16),
+        pltpu.VMEM((MID, OUT), BF16),
+        pltpu.VMEM((OUT, MID), BF16),
+        pltpu.VMEM((TAPS, MID), BF16),
+        pltpu.VMEM((MID, OUT), BF16),
         pltpu.VMEM((ROWS, PIXELS), BF16),
         pltpu.VMEM((TICKS * BLOCK, OUT), BF16),
         pltpu.VMEM((TICKS * BLOCK, TAPS), BF16),
@@ -466,10 +563,14 @@
         pltpu.VMEM((TICKS * BLOCK, MID), BF16),
         pltpu.VMEM((TICKS * BLOCK, MID), BF16),
         pltpu.VMEM((TICKS * BLOCK, OUT), BF16),
+        pltpu.VMEM((TAPS, MID), BF16),
+        pltpu.VMEM((MID, OUT), BF16),
+        pltpu.VMEM((OUT, MID), BF16),
+        pltpu.VMEM((ROWS, TAPS), BF16),
         pltpu.VMEM((3, ROWS + 2 * PITCH, MID), BF16),
         pltpu.VMEM((3, ROWS + 2 * PITCH, MID), BF16),
-        pltpu.VMEM((ROWS, MID), F32),
-        pltpu.VMEM((ROWS, MID), F32),
+        pltpu.VMEM((2, ROWS, MID), F32),
+        pltpu.VMEM((2, ROWS, MID), F32),
         pltpu.VMEM((2, 2 * RANK, MID), BF16),
         pltpu.VMEM((2 * RANK, OUT), BF16),
         pltpu.VMEM((2 * RANK, COLUMNS), F32),
@@ -478,10 +579,11 @@
         pltpu.VMEM((TILED, LANES), F32),
         pltpu.VMEM((TILED // 2, LANES), F32),
         pltpu.VMEM((TILED // 2, LANES), F32),
-        pltpu.VMEM((locals_ - 1, share, LANES), F32),
+        pltpu.VMEM((TILED // 2, LANES), BF16),
+        pltpu.VMEM((locals_ - 1, share, LANES), BF16),
         pltpu.VMEM((across, share, LANES), F32),
-        pltpu.VMEM((TILED, LANES), F32),
-        pltpu.VMEM((2 * RANK, COLUMNS), BF16),
+        pltpu.VMEM((TILED, LANES), BF16),
+        pltpu.VMEM((RANK, COLUMNS), BF16),
         pltpu.VMEM((OUT, LANES), F32),
         pltpu.VMEM((MID, LANES), F32),
         pltpu.VMEM((across, group, LANES), F32),
@@ -489,8 +591,9 @@
         pltpu.VMEM((more, group, LANES), F32),
         pltpu.VMEM((group, LANES), F32),
         pltpu.VMEM((locals_ - 1, e_rows, LANES), F32),
-        dma((TICKS - 1,)),
-        dma((TICKS - 1,)),
+        dma((12,)),
+        dma((TICKS - 1, PIECES)),
+        dma((TICKS - 1, PIECES)),
         dma,
         dma,
         dma((locals_ - 1,)),
@@ -520,7 +623,7 @@
     results = pl.pallas_call(
         functools.partial(kernel, sizes),
         out_shape=shapes,
-        in_specs=[vmem] * 12,
+        in_specs=[hbm] * 9 + [vmem] * 3,
         out_specs=(vmem,) * 7,
         scratch_shapes=scratch,
         compiler_params=pltpu.CompilerParams(
@@ -541,7 +644,9 @@
         prior_spatial[0],
         prior_expand[0],
     )
-    leaving, basis_r, basis_s, *others = results
+    leaving, basis_r, basis_s, *others = pl.pallas_call(
+        hand_over, out_shape=shapes, in_specs=[vmem] * 7, out_specs=(vmem,) * 7
+    )(*results)
     return (leaving[None, None], basis_r.T[None], basis_s[None], *(other.T[None] for other in others))
 
 

time: 87.2 us -> 69.9 us (0.80)
  local copies, waits for them, and re-layouts: 11.4 us -> 2.18 us
  Pallas kernels: 74.7 us -> 66.8 us
    pallas_call x1, Pallas kernels: 74.7 us -> 65.2 us  [on_device(): pl.pallas_call(functools.partial(kernel, sizes), out_shape=shapes, in_spe...]
    unnamed x8 -> x1, local copies, waits for them, and re-layouts: 11.4 us -> 2.18 us
    pallas_call x0 -> x1, Pallas kernels: none -> 1.66 us  [on_device(): pl.pallas_call(hand_over, out_shape=shapes, in_specs=[vmem] * 7, out_spec...]
where the time goes in v2:
time: 69.9 us; the launch traced here: 69.6 us
  Pallas kernels  66.8 us (96%)
  local copies, waits for them, and re-layouts  2.18 us (3%)
    pallas_call x1, Pallas kernels, on_device(): pl.pallas_call(functools.partial(kernel, sizes), out_shape=shapes, in_spe...  65.2 us
    unnamed x1, local copies, waits for them, and re-layouts  2.18 us
    pallas_call x1, Pallas kernels, on_device(): pl.pallas_call(hand_over, out_shape=shapes, in_specs=[vmem] * 7, out_spec...  1.66 us

profile of v2, /device:TPU:64, one launch (start us, length us, event | category | flops | bytes accessed | tf_op | source)
XLA Modules:
  0.0 69.6 jit_solution(16055278337722582383)
XLA Ops:
  0.6 2.2 %copy.21 = bf16[1,1,4,196,512]{4,3,2,1,0:T(8,128)(2,1)} copy(bf16[1,1,4,196,512]{4,2,3,1,0:T(4,128)(2,1)} %param.12) | data formatting | bytes 1605632 | tf_op args[0]
  2.8 65.2 %shard_map.171 = (bf16[196,512]{1,0:T(8,128)(2,1)}, f32[8,32]{1,0:T(8,128)}, f32[32,36]{1,0:T(8,128)}, f32[4,32]{1,0:T(4,128)}, f32[4,32]{1,0:T(4,128)}, /*index=5*/f32[4,32]{1,0:T(4,128)}, f32[8,32]{1,0:T(8,128)}) custom-call(bf16[4,196,512]{2,1,0:T(8,128)(2,1)} %bitcast.31, bf16[196,512]{1,0:T(8,128)(2,1)} %bitcast.39, bf16[3,196,512]{2,1,0:T(8,128)(2,1)} %bitcast.34, ...), custom_call_target="tpu_custom_call" | custom-call | flops 5000000000 | bytes 6000000 | tf_op jit(solution)/shard_map/pallas_call | solution.py:623
  68.0 1.7 %shard_map.172 = (bf16[196,512]{1,0:T(8,128)(2,1)}, f32[8,32]{1,0:T(8,128)}, f32[32,36]{1,0:T(8,128)}, f32[4,32]{1,0:T(4,128)}, f32[4,32]{1,0:T(4,128)}, /*index=5*/f32[4,32]{1,0:T(4,128)}, f32[8,32]{1,0:T(8,128)}) custom-call(bf16[196,512]{1,0:T(8,128)(2,1)} %get-tuple-element.21.refs_0_, f32[8,32]{1,0:T(8,128)} %get-tuple-element.22.refs_1_, ...), custom_call_target="tpu_custom_call" | custom-call | tf_op jit(solution)/shard_map/pallas_call | solution.py:647

commit v3 on v2

--- a/solution.py
+++ b/solution.py
@@ -27,6 +27,31 @@
 F32 = jnp.float32
 BF16 = jnp.bfloat16
 PARTS = ((0, OUT), (OUT, TAPS), (OUT + TAPS, MID))
+
+
+HALF_TILES = COLUMNS // LANES // 2
+HALVES = ((0, OUT // 2), (OUT, TAPS // 2), (OUT + TAPS, MID // 2))
+LATE_TILES = OUT // 2 // LANES
+
+
+def tile_place(tile):
+    place = 0
+    for start, width in HALVES:
+        first, count = start // LANES, width // LANES
+        for half in range(2):
+            inside = (tile >= first + half * count) & (tile < first + (half + 1) * count)
+            here = half * HALF_TILES + place + tile - first - half * count
+            yield inside, here
+        place += count
+
+
+def placed(tile):
+    if isinstance(tile, int):
+        return next(here for inside, here in tile_place(tile) if inside)
+    at = 0
+    for inside, here in tile_place(tile):
+        at = jnp.where(inside, here, at)
+    return at
 
 
 def dot(a, b):
@@ -138,13 +163,10 @@
     y_in,
     x_in,
     full,
-    pt,
     right_tiles,
     right_tmp,
     rc_in,
     r2,
-    rx_in,
-    r3,
     ry_in,
     load_sem,
     relay_send,
@@ -161,8 +183,6 @@
     gc_recv,
     rc_send,
     rc_recv,
-    rx_send,
-    rx_recv,
     ry_send,
     ry_recv,
 ):
@@ -187,6 +207,9 @@
 
     def x_peer(d):
         return (section, lax.rem(column + d, across) * 2 + core, local)
+
+    def plane_peer(dx, dy):
+        return (section, lax.rem(column + dx, across) * 2 + core, lax.rem(local + dy, locals_))
 
     other_core = (section, buddy, local)
 
@@ -212,6 +235,9 @@
         pl.semaphore_signal(barrier, inc=1, device_id=y_peer(d), device_id_type=MESH)
     for d in range(1, across):
         pl.semaphore_signal(barrier, inc=1, device_id=x_peer(d), device_id_type=MESH)
+    for dx in range(1, across):
+        for dy in range(1, locals_):
+            pl.semaphore_signal(barrier, inc=1, device_id=plane_peer(dx, dy), device_id_type=MESH)
 
     def remote(src, dst, send, recv, device):
         return pltpu.make_async_remote_copy(
@@ -291,13 +317,22 @@
         rows = pl.ds(t * BLOCK + first * PITCH, (last - first) * PITCH)
         return (up_all[rows, :].astype(F32) + dot(ga_all[rows, :], wr_t[...])).astype(BF16)
 
-    def left_terms(t):
+    def left_late(t):
         a_r = two_terms(folded(dot_t(prior_rs[0], ga_all[block_of(t), :])))
         acc[:, :OUT] += dot(a_r, x_all[block_of(t), :])
+
+    def left_early(t):
         a_s = two_terms(folded(dot_t(prior_rs[1], gb_all[block_of(t), :])))
         acc[:, OUT : OUT + TAPS] += dot(a_s, cols[block_of(t), :])
         a_e = two_terms(folded(dot_t(prior_e[...], up_all[block_of(t), :])))
         acc[:, OUT + TAPS :] += dot(a_e, h2_all[block_of(t), :])
+
+    def fill(tiles):
+        for j in tiles:
+            at = placed(j) * RANK
+            tiled[at : at + RANK, :] = (
+                acc[:RANK, j * LANES : (j + 1) * LANES] + acc[RANK:, j * LANES : (j + 1) * LANES]
+            )
 
     def piece(t, part):
         first = CUTS[part] - t if part else 0
@@ -341,7 +376,16 @@
                 acc[:, OUT : OUT + TAPS] = dot_t(prior_rs[1], es[...])
                 acc[:, OUT + TAPS :] = dot_t(prior_e[...], ee[...])
             up_all[rows_of(t + 1), :] = dot(spread[...], loss[t]).astype(BF16)
-            left_terms(t)
+            left_late(t)
+            left_early(t)
+
+    mine = pl.ds(pl.multiple_of(core * half_rows, half_rows), half_rows)
+    late = LATE_TILES * RANK
+    to_core = []
+    for i, (first, count) in enumerate(((late, half_rows - late), (0, late))):
+        theirs = pl.ds(pl.multiple_of((1 - core) * half_rows + first, RANK), count)
+        there = core_in.at[first : first + count]
+        to_core.append(remote(tiled.at[theirs], there, core_send.at[i], core_recv.at[i], other_core))
 
     for t in range(TICKS):
         for part in range(PIECES):
@@ -350,27 +394,24 @@
                 gb_rows(t, *piece(t - 1, part))
             elif part == 0:
                 gb_rows(t, 0, SIDE)
+            if t == TICKS - 1 and part == PIECES - 1:
+                left_early(t)
+                fill(range(OUT // LANES, COLUMNS // LANES))
+                to_core[0].start()
             ga_rows(t, *piece(t, part))
             if t < TICKS - 1:
                 first, last = piece(t, part)
                 sent[t, first * PITCH : last * PITCH, :] = dx_rows(t, first, last)
                 if t == 0 and part == 0:
-                    pl.semaphore_wait(barrier, locals_ + across)
+                    pl.semaphore_wait(barrier, locals_ * across + 1)
                 relay[t, part].start()
                 shadow(t, part)
-    left_terms(TICKS - 1)
-
-    for j in range(COLUMNS // LANES):
-        tiled[j * RANK : (j + 1) * RANK, :] = (
-            acc[:RANK, j * LANES : (j + 1) * LANES] + acc[RANK:, j * LANES : (j + 1) * LANES]
-        )
-
-    mine = pl.ds(pl.multiple_of(core * half_rows, half_rows), half_rows)
-    theirs = pl.ds(pl.multiple_of((1 - core) * half_rows, half_rows), half_rows)
-    to_core = remote(tiled.at[theirs], core_in, core_send, core_recv, other_core)
-    to_core.start()
+    left_late(TICKS - 1)
+    fill(range(OUT // LANES))
+    to_core[1].start()
     leaving_ref[...] = dot(gather_matrix(), dx_rows(TICKS - 1, 0, SIDE)).astype(BF16)
-    to_core.wait_recv()
+    for copy in to_core:
+        copy.wait_recv()
     half[...] = tiled[mine, :] + core_in[...]
     half_out[...] = half[...].astype(BF16)
     to_y = []
@@ -406,16 +447,27 @@
         copy.wait_recv()
     from_core = remote(full.at[mine], full.at[mine], gc_send, gc_recv, other_core)
     from_core.start()
+
+    def half_products(which):
+        tiles = []
+        for i in range(HALF_TILES):
+            at = pl.multiple_of(which * half_rows + i * RANK, RANK)
+            tiles.append(full[pl.ds(at, RANK), :])
+        results = []
+        first = 0
+        for (_, width), inputs, errors in zip(HALVES, (x_all, cols, h2_all), (er, es, ee)):
+            terms = jnp.concatenate(tiles[first : first + width // LANES], axis=1)
+            first += width // LANES
+            span = pl.ds(pl.multiple_of(which * width, LANES), width)
+            results += [dot_t(terms, inputs[:, span]), dot(terms, errors[span, :]), dot_t(terms, terms)]
+        return results
+
+    products = half_products(core)
     from_core.wait_recv()
-
-    for j in range(COLUMNS // LANES):
-        pt[:, j * LANES : (j + 1) * LANES] = full[j * RANK : (j + 1) * RANK, :]
-    b_r = two_terms(dot_t(pt[:, :OUT], x_all[...]))
-    sum_r = folded(dot(b_r, ga_all[...])) + dot(pt[:, :OUT], er[...])
-    b_s = two_terms(dot_t(pt[:, OUT : OUT + TAPS], cols[...]))
-    sum_s = folded(dot(b_s, gb_all[...])) + dot(pt[:, OUT : OUT + TAPS], es[...])
-    b_e = two_terms(dot_t(pt[:, OUT + TAPS :], h2_all[...]))
-    sum_e = folded(dot(b_e, up_all[...])) + dot(pt[:, OUT + TAPS :], ee[...])
+    products = [a + b for a, b in zip(products, half_products(1 - core))]
+    sum_r = folded(dot(two_terms(products[0]), ga_all[...])) + products[1]
+    sum_s = folded(dot(two_terms(products[3]), gb_all[...])) + products[4]
+    sum_e = folded(dot(two_terms(products[6]), up_all[...])) + products[7]
     right_tiles[...] = jnp.concatenate([sum_e, jnp.zeros((LANES - RANK, OUT), F32)], axis=0).T
     zero = jnp.zeros((RANK, MID), F32)
     right_tmp[...] = jnp.concatenate([zero, sum_r, sum_s, zero], axis=0).T
@@ -434,13 +486,9 @@
         )
         to_core2[-1].start()
 
-    def gram(start, width):
-        terms = pt[:, start : start + width]
-        return dot_t(terms, terms)
-
     row_id = lax.broadcasted_iota(jnp.int32, (RANK, RANK), 0)
     col_id = lax.broadcasted_iota(jnp.int32, (RANK, RANK), 1)
-    left = [gram(*part) for part in PARTS]
+    left = [products[2], products[5], products[8]]
     inverse = [jnp.where(row_id == col_id, 1.0, 0.0) for _ in PARTS]
 
     def eliminate(steps):
@@ -456,27 +504,17 @@
         copy.wait_recv()
     for i in range(across):
         r2[i] = right_tiles[group_at(i, core), :] + rc_in[i]
-    to_x2 = []
-    for d in range(1, across):
-        to_x2.append(
-            remote(r2.at[lax.rem(column + d, across)], rx_in.at[d - 1], rx_send.at[d - 1], rx_recv.at[d - 1], x_peer(d))
-        )
-        to_x2[-1].start()
-    eliminate(range(RANK // 2))
-    for copy in to_x2:
-        copy.wait_recv()
-    total = r2[column]
-    for d in range(across - 1):
-        total = total + rx_in[d]
-    r3[...] = total
-    to_y2 = []
-    for d in range(1, locals_):
-        at = pl.multiple_of(lax.rem(local + d, locals_) * e_rows, e_rows)
-        to_y2.append(
-            remote(r3.at[pl.ds(at, e_rows)], ry_in.at[d - 1], ry_send.at[d - 1], ry_recv.at[d - 1], y_peer(d))
-        )
-        to_y2[-1].start()
-    eliminate(range(RANK // 2, RANK))
+    to_plane = []
+    for dx in range(across):
+        for dy in range(locals_):
+            if dx + dy > 0:
+                at = pl.multiple_of(lax.rem(local + dy, locals_) * e_rows, e_rows)
+                source = r2.at[lax.rem(column + dx, across), pl.ds(at, e_rows)]
+                slot = dx * locals_ + dy - 1
+                sems = (ry_send.at[slot], ry_recv.at[slot])
+                to_plane.append(remote(source, ry_in.at[slot], *sems, plane_peer(dx, dy)))
+                to_plane[-1].start()
+    eliminate(range(RANK))
     for m in range(3):
         pivots = jnp.sum(jnp.where(row_id == col_id, left[m], 0.0), axis=1, keepdims=True)
         inverse[m] = inverse[m] * lax.rsqrt(pivots)
@@ -491,7 +529,7 @@
         pieces = []
         for i in range(tiles):
             j = jnp.minimum(first + i, COLUMNS // LANES - 1)
-            pieces.append(full[pl.ds(pl.multiple_of(j * RANK, RANK), RANK), :].astype(F32))
+            pieces.append(full[pl.ds(pl.multiple_of(placed(j) * RANK, RANK), RANK), :].astype(F32))
         window = pieces[0] if tiles == 1 else jnp.concatenate(pieces, axis=1)
         span = tiles * LANES
         window = pltpu.roll(window, lax.rem(span - (at - first * LANES), span), 1)
@@ -500,18 +538,18 @@
         else:
             ref[...] = precise_dot_t(window.T[:width, :], inverse[m]) * math.sqrt(rows)
 
-    for copy in to_y2:
+    for copy in to_plane:
         copy.wait_recv()
-    total = r3[pl.ds(pl.multiple_of(local * e_rows, e_rows), e_rows), :]
-    for d in range(locals_ - 1):
-        total = total + ry_in[d]
+    total = r2[column, pl.ds(pl.multiple_of(local * e_rows, e_rows), e_rows), :]
+    for slot in range(across * locals_ - 1):
+        total = total + ry_in[slot]
     right_e_ref[...] = precise_dot_t(total[:, :RANK], inverse[2]) / (replicas * math.sqrt(MID))
     few = total[:, RANK : 2 * RANK]
     right_r_ref[...] = precise_dot_t(few, inverse[0])[:r_rows, :] / (replicas * math.sqrt(OUT))
     few = total[:, 2 * RANK : 3 * RANK]
     right_s_ref[...] = precise_dot_t(few, inverse[1])[:r_rows, :] / (replicas * math.sqrt(TAPS))
 
-    for copy in (*relay.values(), to_core, *to_y, *to_x, *from_y, from_core, *to_core2, *to_x2, *to_y2):
+    for copy in (*relay.values(), *to_core, *to_y, *to_x, *from_y, from_core, *to_core2, *to_plane):
         copy.wait_send()
 
 
@@ -583,19 +621,16 @@
         pltpu.VMEM((locals_ - 1, share, LANES), BF16),
         pltpu.VMEM((across, share, LANES), F32),
         pltpu.VMEM((TILED, LANES), BF16),
-        pltpu.VMEM((RANK, COLUMNS), BF16),
         pltpu.VMEM((OUT, LANES), F32),
         pltpu.VMEM((MID, LANES), F32),
         pltpu.VMEM((across, group, LANES), F32),
         pltpu.VMEM((across, group, LANES), F32),
-        pltpu.VMEM((more, group, LANES), F32),
-        pltpu.VMEM((group, LANES), F32),
-        pltpu.VMEM((locals_ - 1, e_rows, LANES), F32),
+        pltpu.VMEM((across * locals_ - 1, e_rows, LANES), F32),
         dma((12,)),
         dma((TICKS - 1, PIECES)),
         dma((TICKS - 1, PIECES)),
-        dma,
-        dma,
+        dma((2,)),
+        dma((2,)),
         dma((locals_ - 1,)),
         dma((locals_ - 1,)),
         dma((more,)),
@@ -606,10 +641,8 @@
         dma,
         dma((across,)),
         dma((across,)),
-        dma((more,)),
-        dma((more,)),
-        dma((locals_ - 1,)),
-        dma((locals_ - 1,)),
+        dma((across * locals_ - 1,)),
+        dma((across * locals_ - 1,)),
     ]
     shapes = (
         jax.ShapeDtypeStruct((PIXELS, OUT), BF16),

time: 69.9 us -> 68.3 us (0.977)
  Pallas kernels: 66.8 us -> 65.2 us
    pallas_call x1, Pallas kernels: 65.2 us -> 63.6 us  [on_device(): pl.pallas_call(functools.partial(kernel, sizes), out_shape=shapes, in_spe...]
where the time goes in v3:
time: 68.3 us; the launch traced here: 68.1 us
  Pallas kernels  65.2 us (95%)
  local copies, waits for them, and re-layouts  2.18 us (3%)
    pallas_call x1, Pallas kernels, on_device(): pl.pallas_call(functools.partial(kernel, sizes), out_shape=shapes, in_spe...  63.6 us
    unnamed x1, local copies, waits for them, and re-layouts  2.18 us
    pallas_call x1, Pallas kernels, on_device(): pl.pallas_call(hand_over, out_shape=shapes, in_specs=[vmem] * 7, out_spec...  1.66 us

profile of v3, /device:TPU:64, one launch (start us, length us, event | category | flops | bytes accessed | tf_op | source)
XLA Modules:
  0.0 68.1 jit_solution(661022207173677126)
XLA Ops:
  0.6 2.2 %copy.21 = bf16[1,1,4,196,512]{4,3,2,1,0:T(8,128)(2,1)} copy(bf16[1,1,4,196,512]{4,2,3,1,0:T(4,128)(2,1)} %param.12) | data formatting | bytes 1605632 | tf_op args[0]
  2.8 63.6 %shard_map.171 = (bf16[196,512]{1,0:T(8,128)(2,1)}, f32[8,32]{1,0:T(8,128)}, f32[32,36]{1,0:T(8,128)}, f32[4,32]{1,0:T(4,128)}, f32[4,32]{1,0:T(4,128)}, /*index=5*/f32[4,32]{1,0:T(4,128)}, f32[8,32]{1,0:T(8,128)}) custom-call(bf16[4,196,512]{2,1,0:T(8,128)(2,1)} %bitcast.31, bf16[196,512]{1,0:T(8,128)(2,1)} %bitcast.39, bf16[3,196,512]{2,1,0:T(8,128)(2,1)} %bitcast.34, ...), custom_call_target="tpu_custom_call" | custom-call | flops 5000000000 | bytes 6000000 | tf_op jit(solution)/shard_map/pallas_call | solution.py:656
  66.4 1.7 %shard_map.172 = (bf16[196,512]{1,0:T(8,128)(2,1)}, f32[8,32]{1,0:T(8,128)}, f32[32,36]{1,0:T(8,128)}, f32[4,32]{1,0:T(4,128)}, f32[4,32]{1,0:T(4,128)}, /*index=5*/f32[4,32]{1,0:T(4,128)}, f32[8,32]{1,0:T(8,128)}) custom-call(bf16[196,512]{1,0:T(8,128)(2,1)} %get-tuple-element.21.refs_0_, f32[8,32]{1,0:T(8,128)} %get-tuple-element.22.refs_1_, ...), custom_call_target="tpu_custom_call" | custom-call | tf_op jit(solution)/shard_map/pallas_call | solution.py:680

commit v4 on v3

--- a/solution.py
+++ b/solution.py
@@ -214,12 +214,11 @@
     other_core = (section, buddy, local)
 
     pairs = (
-        (x_ref.at[0], x.at[0]),
+        (x_ref, x),
         (wr_ref, wr),
         (ws_ref, ws),
         (grad_ref, grad),
         (we_ref, we),
-        *((x_ref.at[t], x.at[t]) for t in range(1, TICKS)),
         (er_ref, er),
         (es_ref, es),
         (ee_ref, ee),
@@ -269,7 +268,7 @@
         return pl.ds(t * BLOCK, BLOCK)
 
     def forward_one(t):
-        x_all[rows_of(t), :] = dot(spread[...], x[t]).astype(BF16)
+        x_all[rows_of(t), :] = dot(spread[...], x[:, t, :]).astype(BF16)
         pre1 = dot(x_all[rows_of(t), :], wr[...])
         q1 = sigmoid(pre1)
         pixel = lax.broadcasted_iota(jnp.int32, (ROWS, MID), 0) % PITCH < SIDE
@@ -365,13 +364,13 @@
 
     def shadow(t, part):
         if part == 0:
-            arrive(8)
+            arrive(5)
             forward_one(t + 1)
         elif part == 1:
             forward_two(t + 1)
         else:
             if t == 0:
-                arrive(12)
+                arrive(9)
                 acc[:, :OUT] = dot_t(prior_rs[0], er[...])
                 acc[:, OUT : OUT + TAPS] = dot_t(prior_rs[1], es[...])
                 acc[:, OUT + TAPS :] = dot_t(prior_e[...], ee[...])
@@ -409,7 +408,6 @@
     left_late(TICKS - 1)
     fill(range(OUT // LANES))
     to_core[1].start()
-    leaving_ref[...] = dot(gather_matrix(), dx_rows(TICKS - 1, 0, SIDE)).astype(BF16)
     for copy in to_core:
         copy.wait_recv()
     half[...] = tiled[mine, :] + core_in[...]
@@ -421,6 +419,7 @@
             remote(half_out.at[pl.ds(at, share)], y_in.at[d - 1], y_send.at[d - 1], y_recv.at[d - 1], y_peer(d))
         )
         to_y[-1].start()
+    leaving_ref[...] = dot(gather_matrix(), dx_rows(TICKS - 1, 0, SIDE)).astype(BF16)
     for copy in to_y:
         copy.wait_recv()
     summed = half[pl.ds(pl.multiple_of(local * share, share), share), :]
@@ -585,7 +584,7 @@
     more = max(across - 1, 1)
     hbm = pl.BlockSpec(memory_space=pltpu.HBM)
     scratch = [
-        pltpu.VMEM((TICKS, PIXELS, OUT), BF16),
+        pltpu.VMEM((PIXELS, TICKS, OUT), BF16),
         pltpu.VMEM((PIXELS, OUT), BF16),
         pltpu.VMEM((TICKS - 1, PIXELS, OUT), BF16),
         pltpu.VMEM((OUT, MID), BF16),
@@ -626,7 +625,7 @@
         pltpu.VMEM((across, group, LANES), F32),
         pltpu.VMEM((across, group, LANES), F32),
         pltpu.VMEM((across * locals_ - 1, e_rows, LANES), F32),
-        dma((12,)),
+        dma((9,)),
         dma((TICKS - 1, PIECES)),
         dma((TICKS - 1, PIECES)),
         dma((2,)),
@@ -664,7 +663,7 @@
         ),
         cost_estimate=pl.CostEstimate(flops=5_000_000_000, bytes_accessed=6_000_000, transcendentals=500_000),
     )(
-        section_inputs[0, 0],
+        section_inputs[0, 0].transpose(1, 0, 2),
         grad_in[0, 0],
         loss_grad[0],
         w_reduce[0],

time: 68.3 us -> 66.2 us (0.969)
  local copies, waits for them, and re-layouts: 2.18 us -> 0 us
    unnamed x1 -> x0, local copies, waits for them, and re-layouts: 2.18 us -> none
where the time goes in v4:
time: 66.2 us; the launch traced here: 66 us
  Pallas kernels  65.4 us (99%)
    pallas_call x1, Pallas kernels, on_device(): pl.pallas_call(functools.partial(kernel, sizes), out_shape=shapes, in_spe...  63.7 us
    pallas_call x1, Pallas kernels, on_device(): pl.pallas_call(hand_over, out_shape=shapes, in_specs=[vmem] * 7, out_spec...  1.66 us

profile of v4, /device:TPU:64, one launch (start us, length us, event | category | flops | bytes accessed | tf_op | source)
XLA Modules:
  0.0 66.0 jit_solution(5010833923660221657)
XLA Ops:
  0.6 63.7 %shard_map.171 = (bf16[196,512]{1,0:T(8,128)(2,1)}, f32[8,32]{1,0:T(8,128)}, f32[32,36]{1,0:T(8,128)}, f32[4,32]{1,0:T(4,128)}, f32[4,32]{1,0:T(4,128)}, /*index=5*/f32[4,32]{1,0:T(4,128)}, f32[8,32]{1,0:T(8,128)}) custom-call(bf16[196,4,512]{2,1,0:T(4,128)(2,1)} %bitcast.33, bf16[196,512]{1,0:T(8,128)(2,1)} %bitcast.39, bf16[3,196,512]{2,1,0:T(8,128)(2,1)} %bitcast.34, ...), custom_call_target="tpu_custom_call" | custom-call | flops 5000000000 | bytes 6000000 | tf_op jit(solution)/shard_map/pallas_call | solution.py:655
  64.3 1.7 %shard_map.172 = (bf16[196,512]{1,0:T(8,128)(2,1)}, f32[8,32]{1,0:T(8,128)}, f32[32,36]{1,0:T(8,128)}, f32[4,32]{1,0:T(4,128)}, f32[4,32]{1,0:T(4,128)}, /*index=5*/f32[4,32]{1,0:T(4,128)}, f32[8,32]{1,0:T(8,128)}) custom-call(bf16[196,512]{1,0:T(8,128)(2,1)} %get-tuple-element.21.refs_0_, f32[8,32]{1,0:T(8,128)} %get-tuple-element.22.refs_1_, ...), custom_call_target="tpu_custom_call" | custom-call | tf_op jit(solution)/shard_map/pallas_call | solution.py:679

commit v5 on v4

--- a/solution.py
+++ b/solution.py
@@ -553,8 +553,11 @@
 
 
 def hand_over(*refs):
-    for source, target in zip(refs[:7], refs[7:]):
-        target[...] = source[...]
+    copies = [pltpu.make_async_copy(refs[i], refs[7 + i], refs[14].at[i]) for i in range(7)]
+    for copy in copies:
+        copy.start()
+    for copy in copies:
+        copy.wait()
 
 
 def on_device(
@@ -677,7 +680,7 @@
         prior_expand[0],
     )
     leaving, basis_r, basis_s, *others = pl.pallas_call(
-        hand_over, out_shape=shapes, in_specs=[vmem] * 7, out_specs=(vmem,) * 7
+        hand_over, out_shape=shapes, in_specs=[hbm] * 7, out_specs=(hbm,) * 7, scratch_shapes=[dma((7,))]
     )(*results)
     return (leaving[None, None], basis_r.T[None], basis_s[None], *(other.T[None] for other in others))
 

time: 66.2 us -> 73 us (1.10)
  Pallas kernels: 65.4 us -> 72 us
    pallas_call x1, Pallas kernels: 1.66 us -> 8.3 us  [on_device(): pl.pallas_call(hand_over, out_shape=shapes, in_specs=[hbm] * 7, out_specs...]
where the time goes in v5:
time: 73 us; the launch traced here: 72.8 us
  Pallas kernels  72 us (99%)
  between operations  0.81 us (1%)
    pallas_call x1, Pallas kernels, on_device(): pl.pallas_call(functools.partial(kernel, sizes), out_shape=shapes, in_spe...  63.7 us
    pallas_call x1, Pallas kernels, on_device(): pl.pallas_call(hand_over, out_shape=shapes, in_specs=[hbm] * 7, out_specs...  8.3 us

profile of v5, /device:TPU:64, one launch (start us, length us, event | category | flops | bytes accessed | tf_op | source)
XLA Modules:
  0.0 72.8 jit_solution(7319363466002580060)
XLA Ops:
  0.6 63.7 %shard_map.171 = (bf16[196,512]{1,0:T(8,128)(2,1)}, f32[8,32]{1,0:T(8,128)}, f32[32,36]{1,0:T(8,128)}, f32[4,32]{1,0:T(4,128)}, f32[4,32]{1,0:T(4,128)}, /*index=5*/f32[4,32]{1,0:T(4,128)}, f32[8,32]{1,0:T(8,128)}) custom-call(bf16[196,4,512]{2,1,0:T(4,128)(2,1)} %bitcast.33, bf16[196,512]{1,0:T(8,128)(2,1)} %bitcast.39, bf16[3,196,512]{2,1,0:T(8,128)(2,1)} %bitcast.34, ...), custom_call_target="tpu_custom_call" | custom-call | flops 5000000000 | bytes 6000000 | tf_op jit(solution)/shard_map/pallas_call | solution.py:658
  64.3 8.3 %shard_map.172 = (bf16[196,512]{1,0:T(8,128)(2,1)}, f32[8,32]{1,0:T(8,128)}, f32[32,36]{1,0:T(8,128)}, f32[4,32]{1,0:T(4,128)}, f32[4,32]{1,0:T(4,128)}, /*index=5*/f32[4,32]{1,0:T(4,128)}, f32[8,32]{1,0:T(8,128)}) custom-call(bf16[196,512]{1,0:T(8,128)(2,1)} %get-tuple-element.21.refs_0_, f32[8,32]{1,0:T(8,128)} %get-tuple-element.22.refs_1_, ...), custom_call_target="tpu_custom_call" | custom-call | tf_op jit(solution)/shard_map/pallas_call | solution.py:682
